TPU v7x, 512 devices: a whole 4x4x16 slice. The times are simulated.
512 devices in a mesh: segment: 2 (over core), row: 16 (over z_lo, y), col: 16 (over z_hi, x).
Axes of the slice: x: 4, y: 4, z: 16 (z_hi: 4, z_lo: 4; z = z_hi * 4 + z_lo), core: 2. Of those that a mesh axis runs over, the one named last changes fastest.
Arguments:
- activations: bfloat16 [2, 384, 384, 128], P('segment', 'row', 'col'), may hold values from -6 to 6
- cotangent: bfloat16 [2, 384, 384, 128], P('segment', 'row', 'col'), may hold values from -6 to 6
- conv_weight: bfloat16 [2, 9, 128, 64], P('segment'), may hold values from -0.1875 to 0.1875
- conv_bias: bfloat16 [2, 64], P('segment'), may hold values from -3 to 3
- out_weight: bfloat16 [2, 64, 128], P('segment'), may hold values from -0.75 to 0.75
Outputs:
- input_gradient: bfloat16 [2, 384, 384, 128], P('segment', 'row', 'col')
- conv_gradient: float32 [2, 9, 128, 64], P('segment')
- bias_gradient: float32 [2, 64], P('segment')
- output_weight_gradient: float32 [2, 64, 128], P('segment')
All inputs are finite; a program needn't handle non-finite values.
Results may differ from a plain program's by a relative error of at most 0.022.
The roundings to bfloat16 on the way count: a program that leaves them out, or rounds other values in their place, can miss the bound.
Values may be sent and summed in bfloat16 or wider, within the bound.
A program may use at most 64 MiB of HBM per device.

v0:
```python
import jax
import jax.numpy as jnp
from jax import lax
from jax.sharding import PartitionSpec as P

FIRST_DILATION = 2
SECOND_DILATION = 8


def extended(x, sides, width):
    for axis, dim in sides:
        count, length = (lax.axis_size(axis), x.shape[dim])
        up = [(i, (i + 1) % count) for i in range(count - 1)]
        down = [(j, i) for i, j in up]
        last = lax.slice_in_dim(x, length - width, length, axis=dim)
        first = lax.slice_in_dim(x, 0, width, axis=dim)
        before = lax.ppermute(last, axis, up)
        after = lax.ppermute(first, axis, down)
        x = jnp.concatenate([before, x, after], axis=dim)
    return x


def tap_window(padded, dilation, row_offset_tap, col_tap, side):
    row_start = dilation * (1 + row_offset_tap)
    col_start = dilation * (1 + col_tap)
    return padded[row_start : row_start + side, col_start : col_start + side]


def mirror(square):
    number = lax.axis_size("row")
    groups = square.reshape(square.shape[0], square.shape[1], number, square.shape[2] // number)
    groups = lax.all_to_all(groups, "col", split_axis=2, concat_axis=2, tiled=True)
    groups = lax.all_to_all(groups, "row", split_axis=2, concat_axis=2, tiled=True)
    groups = lax.all_to_all(groups, "col", split_axis=2, concat_axis=2, tiled=True)
    current = groups.reshape(square.shape)
    return jnp.swapaxes(current, 0, 1)


def forward_section(inputs, conv, bias, projection, dilation):
    side = inputs.shape[0]
    channels = inputs.shape[2]
    hidden = jnp.maximum(inputs, 0)
    padded = extended(hidden, (("row", 0), ("col", 1)), dilation)
    summed = jnp.zeros((side * side, conv.shape[2]), jnp.float32)
    for tap_index in range(9):
        window = tap_window(padded, dilation, tap_index // 3 - 1, tap_index % 3 - 1, side)
        summed = summed + jnp.dot(
            window.reshape(-1, channels), conv[tap_index], preferred_element_type=jnp.float32
        )
    pre_act = summed + bias.astype(jnp.float32)
    bottle = jnp.maximum(pre_act, 0.0).astype(jnp.bfloat16)
    branch_sum = (
        (
            inputs.reshape(-1, channels).astype(jnp.float32)
            + jnp.dot(bottle, projection, preferred_element_type=jnp.float32)
        )
        .astype(jnp.bfloat16)
        .reshape(side, side, channels)
    )
    mirrored = mirror(branch_sum)
    sym = ((branch_sum.astype(jnp.float32) + mirrored.astype(jnp.float32)) * 0.5).astype(
        jnp.bfloat16
    )
    return (sym, (inputs, padded, pre_act, bottle))


def backward_section(upstream, stored, conv, projection, dilation):
    inputs, padded, pre_act, bottle = stored
    side = inputs.shape[0]
    channels = inputs.shape[2]
    mirrored = mirror(upstream)
    grad_branch = (
        ((upstream.astype(jnp.float32) + mirrored.astype(jnp.float32)) * 0.5)
        .astype(jnp.bfloat16)
        .reshape(-1, channels)
    )
    grad_bottle = lax.dot_general(
        grad_branch, projection, (((1,), (1,)), ((), ())), preferred_element_type=jnp.float32
    )
    grad_pre = jnp.where(pre_act > 0, grad_bottle, 0.0).astype(jnp.bfloat16)
    grad_proj = lax.dot_general(
        bottle, grad_branch, (((0,), (0,)), ((), ())), preferred_element_type=jnp.float32
    )
    grad_bias = jnp.sum(grad_pre.astype(jnp.float32), axis=0)
    conv_terms = []
    for tap_index in range(9):
        window = tap_window(padded, dilation, tap_index // 3 - 1, tap_index % 3 - 1, side)
        conv_terms.append(
            lax.dot_general(
                window.reshape(-1, channels),
                grad_pre,
                (((0,), (0,)), ((), ())),
                preferred_element_type=jnp.float32,
            )
        )
    grad_conv = jnp.stack(conv_terms)
    grad_square = grad_pre.reshape(side, side, -1)
    grad_padded = extended(grad_square, (("row", 0), ("col", 1)), dilation)
    summed = jnp.zeros((side * side, channels), jnp.float32)
    for tap_index in range(9):
        window = tap_window(grad_padded, dilation, 1 - tap_index // 3, 1 - tap_index % 3, side)
        summed = summed + lax.dot_general(
            window.reshape(-1, window.shape[2]),
            conv[tap_index],
            (((1,), (1,)), ((), ())),
            preferred_element_type=jnp.float32,
        )
    masked = jnp.where(inputs.reshape(-1, channels) > 0, summed, 0.0)
    grad_inputs = (
        (grad_branch.astype(jnp.float32) + masked)
        .astype(jnp.bfloat16)
        .reshape(side, side, channels)
    )
    return (grad_inputs, (grad_conv, grad_bias, grad_proj))


def local(activations, cotangent, conv_weight, conv_bias, out_weight):
    every_convolution, all_bias, all_proj = (
        lax.all_gather(conv_weight, "segment", axis=0, tiled=True),
        lax.all_gather(conv_bias, "segment", axis=0, tiled=True),
        lax.all_gather(out_weight, "segment", axis=0, tiled=True),
    )
    dilation_list = (FIRST_DILATION, SECOND_DILATION)
    current = activations[0]
    stored_list = []
    for section in range(2):
        current, stored = forward_section(
            current,
            every_convolution[section],
            all_bias[section],
            all_proj[section],
            dilation_list[section],
        )
        stored_list.append(stored)
    upstream = cotangent[0]
    conv_list = [None, None]
    bias_list = [None, None]
    proj_list = [None, None]
    for section in (1, 0):
        upstream, section_grads = backward_section(
            upstream,
            stored_list[section],
            every_convolution[section],
            all_proj[section],
            dilation_list[section],
        )
        conv_list[section] = section_grads[0]
        bias_list[section] = section_grads[1]
        proj_list[section] = section_grads[2]
    conv_both = jnp.stack(conv_list)
    bias_both = jnp.stack(bias_list)
    proj_both = jnp.stack(proj_list)
    convolution_sum, bias_sum, projection_sum = lax.psum(
        (conv_both, bias_both, proj_both), ("segment", "row", "col")
    )
    own_segment = lax.axis_index("segment")
    convolution_sum = lax.dynamic_slice_in_dim(convolution_sum, own_segment, 1, 0)
    bias_sum = lax.dynamic_slice_in_dim(bias_sum, own_segment, 1, 0)
    projection_sum = lax.dynamic_slice_in_dim(projection_sum, own_segment, 1, 0)
    side = activations.shape[1]
    cells = lax.axis_size("segment") * (side * lax.axis_size("row")) * (side * lax.axis_size("col"))
    factor = 1.0 / jnp.sqrt(jnp.float32(cells))
    return (upstream[None], convolution_sum * factor, bias_sum * factor, projection_sum * factor)


def solution(mesh):
    in_specs = (
        P("segment", "row", "col", None),
        P("segment", "row", "col", None),
        P("segment", None, None, None),
        P("segment", None),
        P("segment", None, None),
    )
    out_specs = (
        P("segment", "row", "col", None),
        P("segment", None, None, None),
        P("segment", None),
        P("segment", None, None),
    )
    return jax.shard_map(local, mesh=mesh, in_specs=in_specs, out_specs=out_specs, check_vma=False)
```

profile of v0, /device:TPU:6, one launch (start us, length us, event | category | flops | bytes accessed | tf_op | source)
XLA Modules:
  0.0 864.9 jit_solution(2562210616461370350)
XLA Ops:
  8.1 3.5 collective-permute-start
  14.4 1.7 reshape.270
  16.1 18.0 %all-to-all-start = ((bf16[16,2,2304]{2,1,0:T(2,128)(2,1)}), bf16[16,2,2304]{2,1,0:T(2,128)(2,1)S(1)}, u32[]{:S(2)}, u32[]{:S(2)}) async-start(bf16[16,2,2304]{2,1,0:T(2,128)(2,1)} %reshape.270), calls=%async_computation | async-start | bytes 294912 | tf_op jit(solution)/shard_map/all_to_all | solution.py:32
  34.1 1.8 all-gather
  36.4 2.0 all_gather.9
  38.4 1.8 all_gather.11
  40.3 7.3 collective-permute-start.2
  47.6 1.9 collective-permute-start.3
  49.7 9.5 %collective-permute-done.3 = bf16[28,2,128]{2,1,0:T(2,128)(2,1)S(1)} collective-permute-done((bf16[28,2,128]{2,1,0:T(2,128)(2,1)S(1)}, bf16[28,2,128]{2,1,0:T(2,128)(2,1)S(1)}, u32[]{:S(2)}, u32[]{:S(2)}) %collective-permute-start.3) | collective-permute-done | bytes 14368 | tf_op jit(solution)/shard_map/ppermute | solution.py:18
  62.1 1.7 reshape.264
  63.8 9.3 %all-to-all-start.3 = ((bf16[16,2,2304]{2,1,0:T(2,128)(2,1)}), bf16[16,2,2304]{2,1,0:T(2,128)(2,1)S(1)}, u32[]{:S(2)}, u32[]{:S(2)}) async-start(bf16[16,2,2304]{2,1,0:T(2,128)(2,1)} %reshape.264), calls=%async_computation.3 | async-start | bytes 294912 | tf_op jit(solution)/shard_map/all_to_all | solution.py:32
  74.2 1.7 reshape.272
  75.9 12.6 %all-to-all-done.3 = bf16[16,2,2304]{2,1,0:T(2,128)(2,1)S(1)} async-done(((bf16[16,2,2304]{2,1,0:T(2,128)(2,1)}), bf16[16,2,2304]{2,1,0:T(2,128)(2,1)S(1)}, u32[]{:S(2)}, u32[]{:S(2)}) %all-to-all-start.3) | async-done | bytes 147488 | tf_op jit(solution)/shard_map/all_to_all | solution.py:32
  88.5 6.7 all-to-all-start.1
  96.4 1.7 reshape.266
  98.0 6.2 all-to-all-done.1
  104.3 3.5 all-to-all-start.4
  108.9 1.7 reshape.274
  110.6 6.2 all-to-all-done.4
  116.8 5.5 all-to-all-start.2
  123.5 1.7 reshape.268
  125.1 10.6 %all-to-all-done.2 = bf16[16,2,2304]{2,1,0:T(2,128)(2,1)S(1)} async-done(((bf16[16,2,2304]{2,1,0:T(2,128)(2,1)}), bf16[16,2,2304]{2,1,0:T(2,128)(2,1)S(1)}, u32[]{:S(2)}, u32[]{:S(2)}) %all-to-all-start.2) | async-done | bytes 147488 | tf_op jit(solution)/shard_map/all_to_all | solution.py:34
  135.7 6.2 all-to-all-start.5
  144.8 10.5 %all-to-all-done.5 = bf16[16,2,2304]{2,1,0:T(2,128)(2,1)} async-done(((bf16[16,2,2304]{2,1,0:T(2,128)(2,1)}), bf16[16,2,2304]{2,1,0:T(2,128)(2,1)}, u32[]{:S(2)}, u32[]{:S(2)}) %all-to-all-start.5) | async-done | bytes 147488 | tf_op jit(solution)/shard_map/all_to_all | solution.py:34
  155.3 2.0 reshape.269
  158.1 2.4 collective-permute-start.4
  162.5 4.0 collective-permute-done.5
  166.4 3.7 collective-permute-start.6
  170.2 2.1 collective-permute-start.7
  172.8 9.7 %collective-permute-done.7 = bf16[40,8,128]{2,1,0:T(8,128)(2,1)S(1)} collective-permute-done((bf16[40,8,128]{2,1,0:T(8,128)(2,1)S(1)}, bf16[40,8,128]{2,1,0:T(8,128)(2,1)S(1)}, u32[]{:S(2)}, u32[]{:S(2)}) %collective-permute-start.7) | collective-permute-done | bytes 81952 | tf_op jit(solution)/shard_map/ppermute | solution.py:18
  186.8 4.5 collective-permute-start.8
  193.1 1.9 collective-permute-start.10
  195.1 9.9 %collective-permute-start.11 = (bf16[40,8,64]{2,1,0:T(8,128)(2,1)S(1)}, bf16[40,8,64]{2,1,0:T(8,128)(2,1)S(1)}, u32[]{:S(2)}, u32[]{:S(2)}) collective-permute-start(bf16[40,8,64]{2,1,0:T(8,128)(2,1)S(1)} %get-tuple-element.21), channel_id=1, source_target_pairs={{0,1},{1,2},{2,3},{3,4},{4,5},{5,6},{6,7},{7,8},{8,9},{9,10},{10,1... | collective-permute-start | bytes 122888 | tf_op jit(solution)/shard_map/ppermute | solution.py:17
  209.6 1.7 reshape.276
  211.2 12.9 %all-to-all-start.6 = ((bf16[16,2,2304]{2,1,0:T(2,128)(2,1)}), bf16[16,2,2304]{2,1,0:T(2,128)(2,1)S(1)}, u32[]{:S(2)}, u32[]{:S(2)}) async-start(bf16[16,2,2304]{2,1,0:T(2,128)(2,1)} %reshape.276), calls=%async_computation.6 | async-start | bytes 294912 | tf_op jit(solution)/shard_map/all_to_all | solution.py:32
  226.5 11.0 %all-to-all-done.6 = bf16[16,2,2304]{2,1,0:T(2,128)(2,1)S(1)} async-done(((bf16[16,2,2304]{2,1,0:T(2,128)(2,1)}), bf16[16,2,2304]{2,1,0:T(2,128)(2,1)S(1)}, u32[]{:S(2)}, u32[]{:S(2)}) %all-to-all-start.6) | async-done | bytes 147488 | tf_op jit(solution)/shard_map/all_to_all | solution.py:32
  240.3 14.4 %all-to-all-start.7 = ((bf16[16,2,2304]{2,1,0:T(2,128)(2,1)}), bf16[16,2,2304]{2,1,0:T(2,128)(2,1)S(1)}, u32[]{:S(2)}, u32[]{:S(2)}) async-start(bf16[16,2,2304]{2,1,0:T(2,128)(2,1)} %reshape.278), calls=%async_computation.7 | async-start | bytes 294912 | tf_op jit(solution)/shard_map/all_to_all | solution.py:33
  255.4 1.7 fusion.20
  257.9 6.3 all-to-all-done.7
  265.5 1.7 reshape.280
  267.1 5.8 all-to-all-start.8
  275.2 11.1 %all-to-all-done.8 = bf16[16,2,2304]{2,1,0:T(2,128)(2,1)S(1)} async-done(((bf16[16,2,2304]{2,1,0:T(2,128)(2,1)}), bf16[16,2,2304]{2,1,0:T(2,128)(2,1)S(1)}, u32[]{:S(2)}, u32[]{:S(2)}) %all-to-all-start.8) | async-done | bytes 147488 | tf_op jit(solution)/shard_map/all_to_all | solution.py:34
  289.2 98.7 %psum.22 = f32[2,64]{1,0:T(2,128)S(1)} all-reduce(f32[2,64]{1,0:T(2,128)S(1)} %pad_maximum_fusion.26), channel_id=1, replica_groups=mesh['segment'=2,'row'=16,'col'=16] {'segment','row','col'}, use_global_device_ids=true, to_apply=%region_3.4 | all-reduce | flops 128 | bytes 1024 | tf_op jit(solution)/shard_map/psum | solution.py:153
  389.3 4.5 collective-permute-start.12
  397.5 2.6 collective-permute-start.14
  400.1 9.3 %collective-permute-start.15 = (bf16[28,2,64]{2,1,0:T(2,128)(2,1)S(1)}, bf16[28,2,64]{2,1,0:T(2,128)(2,1)S(1)}, u32[]{:S(2)}, u32[]{:S(2)}) collective-permute-start(bf16[28,2,64]{2,1,0:T(2,128)(2,1)S(1)} %get-tuple-element.41), channel_id=1, source_target_pairs={{0,1},{1,2},{2,3},{3,4},{4,5},{5,6},{6,7},{7,8},{8,9},{9,10},{10,1... | collective-permute-start | bytes 21512 | tf_op jit(solution)/shard_map/ppermute | solution.py:17
  413.1 441.8 %all-reduce.3.cloned.1.call-done = (f32[2,9,128,64]{2,3,1,0:T(8,128)}, f32[2,64,128]{2,1,0:T(8,128)}) async-done(((f32[2,9,128,64]{2,3,1,0:T(8,128)}, f32[2,64,128]{2,1,0:T(8,128)}), (f32[2,9,128,64]{2,3,1,0:T(8,128)}, f32[2,64,128]{2,1,0:T(8,128)})) %all-reduce.3.cloned.1.call-update) | async-done | bytes 655376 | tf_op jit(solution)/shard_map/psum | solution.py:153
  855.0 1.7 dynamic-slice_multiply_fusion
  (204 shorter events, 51.2 us)
Async XLA Ops:
  8.1 32.1 %collective-permute-start = (bf16[2,24,128]{2,1,0:T(8,128)(2,1)S(1)}, bf16[2,24,128]{2,1,0:T(8,128)(2,1)S(1)}, u32[]{:S(2)}, u32[]{:S(2)}) collective-permute-start(bf16[2,24,128]{2,1,0:T(8,128)(2,1)S(1)} %get-tuple-element.56), channel_id=1, source_target_pairs={{0,16},{16,32},{32,48},{48,64},{64,80},{80,96},{96,112},{112,128},... | collective-permute-start | bytes 36872 | tf_op jit(solution)/shard_map/ppermute | solution.py:17
  11.6 28.7 %collective-permute-start.1 = (bf16[2,24,128]{2,1,0:T(8,128)(2,1)S(1)}, bf16[2,24,128]{2,1,0:T(8,128)(2,1)S(1)}, u32[]{:S(2)}, u32[]{:S(2)}) collective-permute-start(bf16[2,24,128]{2,1,0:T(8,128)(2,1)S(1)} %get-tuple-element.57), channel_id=1, source_target_pairs={{16,0},{32,16},{48,32},{64,48},{80,64},{96,80},{112,96},{128,112},... | collective-permute-start | bytes 36872 | tf_op jit(solution)/shard_map/ppermute | solution.py:18
  14.2 19.9 %copy-start.28 = (bf16[1,64]{1,0:T(2,128)(2,1)S(1)}, bf16[1,64]{1,0:T(2,128)(2,1)}, u32[]{:S(2)}) copy-start(bf16[1,64]{1,0:T(2,128)(2,1)} %param.8) | copy-start | bytes 388
  14.2 22.2 %copy-start.23 = (bf16[1,9,128,64]{2,3,1,0:T(8,128)(2,1)S(1)}, bf16[1,9,128,64]{2,3,1,0:T(8,128)(2,1)}, u32[]{:S(2)}) copy-start(bf16[1,9,128,64]{2,3,1,0:T(8,128)(2,1)} %param.7) | copy-start | bytes 442372
  14.2 24.2 %copy-start.25 = (bf16[1,64,128]{2,1,0:T(8,128)(2,1)S(1)}, bf16[1,64,128]{2,1,0:T(8,128)(2,1)}, u32[]{:S(2)}) copy-start(bf16[1,64,128]{2,1,0:T(8,128)(2,1)} %param.9) | copy-start | bytes 49156
  16.1 47.7 %all-to-all-start = ((bf16[16,2,2304]{2,1,0:T(2,128)(2,1)}), bf16[16,2,2304]{2,1,0:T(2,128)(2,1)S(1)}, u32[]{:S(2)}, u32[]{:S(2)}) async-start(bf16[16,2,2304]{2,1,0:T(2,128)(2,1)} %reshape.270), calls=%async_computation | async-start | bytes 294912 | tf_op jit(solution)/shard_map/all_to_all | solution.py:32
  40.3 20.8 %copy-start.20 = (bf16[2,64,128]{2,1,0:T(8,128)(2,1)}, bf16[2,64,128]{2,1,0:T(8,128)(2,1)S(1)}, u32[]{:S(2)}) copy-start(bf16[2,64,128]{2,1,0:T(8,128)(2,1)S(1)} %all_gather.11) | copy-start | bytes 98308
  40.3 9.4 %collective-permute-start.2 = (bf16[28,2,128]{2,1,0:T(2,128)(2,1)S(1)}, bf16[28,2,128]{2,1,0:T(2,128)(2,1)S(1)}, u32[]{:S(2)}, u32[]{:S(2)}) collective-permute-start(bf16[28,2,128]{2,1,0:T(2,128)(2,1)S(1)} %get-tuple-element.44), channel_id=1, source_target_pairs={{0,1},{1,2},{2,3},{3,4},{4,5},{5,6},{6,7},{7,8},{8,9},{9,10},{10,1... | collective-permute-start | bytes 43016 | tf_op jit(solution)/shard_map/ppermute | solution.py:17
  47.6 11.6 %collective-permute-start.3 = (bf16[28,2,128]{2,1,0:T(2,128)(2,1)S(1)}, bf16[28,2,128]{2,1,0:T(2,128)(2,1)S(1)}, u32[]{:S(2)}, u32[]{:S(2)}) collective-permute-start(bf16[28,2,128]{2,1,0:T(2,128)(2,1)S(1)} %get-tuple-element.45), channel_id=1, source_target_pairs={{1,0},{2,1},{3,2},{4,3},{5,4},{6,5},{7,6},{8,7},{9,8},{10,9},{11,1... | collective-permute-start | bytes 43016 | tf_op jit(solution)/shard_map/ppermute | solution.py:18
  49.5 11.3 %copy-start.11 = (bf16[24,24,128]{2,1,0:T(8,128)(2,1)}, bf16[24,24,128]{2,1,0:T(8,128)(2,1)S(1)}, u32[]{:S(2)}) copy-start(bf16[24,24,128]{2,1,0:T(8,128)(2,1)S(1)} %get-tuple-element.54) | copy-start | bytes 442372
  59.5 1.3 copy-start
  59.5 1.3 copy-start.2
  59.5 1.3 copy-start.4
  59.5 1.3 copy-start.6
  59.5 1.3 copy-start.8
  63.8 24.8 %all-to-all-start.3 = ((bf16[16,2,2304]{2,1,0:T(2,128)(2,1)}), bf16[16,2,2304]{2,1,0:T(2,128)(2,1)S(1)}, u32[]{:S(2)}, u32[]{:S(2)}) async-start(bf16[16,2,2304]{2,1,0:T(2,128)(2,1)} %reshape.264), calls=%async_computation.3 | async-start | bytes 294912 | tf_op jit(solution)/shard_map/all_to_all | solution.py:32
  88.5 15.7 %all-to-all-start.1 = ((bf16[16,2,2304]{2,1,0:T(2,128)(2,1)}), bf16[16,2,2304]{2,1,0:T(2,128)(2,1)S(1)}, u32[]{:S(2)}, u32[]{:S(2)}) async-start(bf16[16,2,2304]{2,1,0:T(2,128)(2,1)} %reshape.272), calls=%async_computation.1 | async-start | bytes 294912 | tf_op jit(solution)/shard_map/all_to_all | solution.py:33
  104.3 12.5 %all-to-all-start.4 = ((bf16[16,2,2304]{2,1,0:T(2,128)(2,1)}), bf16[16,2,2304]{2,1,0:T(2,128)(2,1)S(1)}, u32[]{:S(2)}, u32[]{:S(2)}) async-start(bf16[16,2,2304]{2,1,0:T(2,128)(2,1)} %reshape.266), calls=%async_computation.4 | async-start | bytes 294912 | tf_op jit(solution)/shard_map/all_to_all | solution.py:33
  116.8 18.9 %all-to-all-start.2 = ((bf16[16,2,2304]{2,1,0:T(2,128)(2,1)}), bf16[16,2,2304]{2,1,0:T(2,128)(2,1)S(1)}, u32[]{:S(2)}, u32[]{:S(2)}) async-start(bf16[16,2,2304]{2,1,0:T(2,128)(2,1)} %reshape.274), calls=%async_computation.2 | async-start | bytes 294912 | tf_op jit(solution)/shard_map/all_to_all | solution.py:34
  135.7 19.6 %all-to-all-start.5 = ((bf16[16,2,2304]{2,1,0:T(2,128)(2,1)}), bf16[16,2,2304]{2,1,0:T(2,128)(2,1)}, u32[]{:S(2)}, u32[]{:S(2)}) async-start(bf16[16,2,2304]{2,1,0:T(2,128)(2,1)} %reshape.268), calls=%async_computation.5 | async-start | bytes 294912 | tf_op jit(solution)/shard_map/all_to_all | solution.py:34
  158.1 4.4 collective-permute-start.4
  160.4 6.0 collective-permute-start.5
  166.4 6.3 collective-permute-start.6
  170.2 12.4 %collective-permute-start.7 = (bf16[40,8,128]{2,1,0:T(8,128)(2,1)S(1)}, bf16[40,8,128]{2,1,0:T(8,128)(2,1)S(1)}, u32[]{:S(2)}, u32[]{:S(2)}) collective-permute-start(bf16[40,8,128]{2,1,0:T(8,128)(2,1)S(1)} %get-tuple-element.25), channel_id=1, source_target_pairs={{1,0},{2,1},{3,2},{4,3},{5,4},{6,5},{7,6},{8,7},{9,8},{10,9},{11,1... | collective-permute-start | bytes 245768 | tf_op jit(solution)/shard_map/ppermute | solution.py:18
  172.3 11.7 %copy-start.14 = (bf16[24,24,128]{2,1,0:T(8,128)(2,1)}, bf16[24,24,128]{2,1,0:T(8,128)(2,1)S(1)}, u32[]{:S(2)}) copy-start(bf16[24,24,128]{2,1,0:T(8,128)(2,1)S(1)} %get-tuple-element.50) | copy-start | bytes 442372
  182.8 24.5 %copy-start.13 = (bf16[24,24,128]{2,1,0:T(8,128)(2,1)}, bf16[24,24,128]{2,1,0:T(8,128)(2,1)S(1)}, u32[]{:S(2)}) copy-start(bf16[24,24,128]{2,1,0:T(8,128)(2,1)S(1)} %get-tuple-element.15) | copy-start | bytes 442372
  182.8 1.3 copy-start.27
  185.5 6.8 collective-permute-start.9
  186.8 6.3 collective-permute-start.8
  193.1 13.3 %collective-permute-start.10 = (bf16[40,8,64]{2,1,0:T(8,128)(2,1)S(1)}, bf16[40,8,64]{2,1,0:T(8,128)(2,1)S(1)}, u32[]{:S(2)}, u32[]{:S(2)}) collective-permute-start(bf16[40,8,64]{2,1,0:T(8,128)(2,1)S(1)} %get-tuple-element.20), channel_id=1, source_target_pairs={{1,0},{2,1},{3,2},{4,3},{5,4},{6,5},{7,6},{8,7},{9,8},{10,9},{11,1... | collective-permute-start | bytes 122888 | tf_op jit(solution)/shard_map/ppermute | solution.py:18
  195.1 12.0 %collective-permute-start.11 = (bf16[40,8,64]{2,1,0:T(8,128)(2,1)S(1)}, bf16[40,8,64]{2,1,0:T(8,128)(2,1)S(1)}, u32[]{:S(2)}, u32[]{:S(2)}) collective-permute-start(bf16[40,8,64]{2,1,0:T(8,128)(2,1)S(1)} %get-tuple-element.21), channel_id=1, source_target_pairs={{0,1},{1,2},{2,3},{3,4},{4,5},{5,6},{6,7},{7,8},{8,9},{9,10},{10,1... | collective-permute-start | bytes 122888 | tf_op jit(solution)/shard_map/ppermute | solution.py:17
  211.2 26.2 %all-to-all-start.6 = ((bf16[16,2,2304]{2,1,0:T(2,128)(2,1)}), bf16[16,2,2304]{2,1,0:T(2,128)(2,1)S(1)}, u32[]{:S(2)}, u32[]{:S(2)}) async-start(bf16[16,2,2304]{2,1,0:T(2,128)(2,1)} %reshape.276), calls=%async_computation.6 | async-start | bytes 294912 | tf_op jit(solution)/shard_map/all_to_all | solution.py:32
  240.3 24.0 %all-to-all-start.7 = ((bf16[16,2,2304]{2,1,0:T(2,128)(2,1)}), bf16[16,2,2304]{2,1,0:T(2,128)(2,1)S(1)}, u32[]{:S(2)}, u32[]{:S(2)}) async-start(bf16[16,2,2304]{2,1,0:T(2,128)(2,1)} %reshape.278), calls=%async_computation.7 | async-start | bytes 294912 | tf_op jit(solution)/shard_map/all_to_all | solution.py:33
  265.4 8.3 copy-start.15
  267.1 19.2 %all-to-all-start.8 = ((bf16[16,2,2304]{2,1,0:T(2,128)(2,1)}), bf16[16,2,2304]{2,1,0:T(2,128)(2,1)S(1)}, u32[]{:S(2)}, u32[]{:S(2)}) async-start(bf16[16,2,2304]{2,1,0:T(2,128)(2,1)} %reshape.280), calls=%async_computation.8 | async-start | bytes 294912 | tf_op jit(solution)/shard_map/all_to_all | solution.py:34
  272.9 582.1 %all-reduce.3.cloned.1.call-start = ((), (), s32[]{:S(2)}) async-start(), calls=%async_computation.9 | async-start | bytes 1310720 | tf_op jit(solution)/shard_map/psum | solution.py:153
  287.6 1.6 copy-start.26
  288.1 105.9 %copy-start.7 = (bf16[24,24,128]{2,1,0:T(8,128)(2,1)S(1)}, bf16[24,24,128]{2,1,0:T(8,128)(2,1)}, u32[]{:S(2)}) copy-start(bf16[24,24,128]{2,1,0:T(8,128)(2,1)} %copy-done.6) | copy-start | bytes 442372
  288.1 106.1 %copy-start.5 = (bf16[24,24,128]{2,1,0:T(8,128)(2,1)S(1)}, bf16[24,24,128]{2,1,0:T(8,128)(2,1)}, u32[]{:S(2)}) copy-start(bf16[24,24,128]{2,1,0:T(8,128)(2,1)} %copy-done.4) | copy-start | bytes 442372
  288.1 106.4 %copy-start.3 = (bf16[24,24,128]{2,1,0:T(8,128)(2,1)S(1)}, bf16[24,24,128]{2,1,0:T(8,128)(2,1)}, u32[]{:S(2)}) copy-start(bf16[24,24,128]{2,1,0:T(8,128)(2,1)} %copy-done.2) | copy-start | bytes 442372
  288.2 106.5 %copy-start.1 = (bf16[24,24,128]{2,1,0:T(8,128)(2,1)S(1)}, bf16[24,24,128]{2,1,0:T(8,128)(2,1)}, u32[]{:S(2)}) copy-start(bf16[24,24,128]{2,1,0:T(8,128)(2,1)} %copy-done) | copy-start | bytes 442372
  288.2 106.7 %copy-start.12 = (bf16[24,24,128]{2,1,0:T(8,128)(2,1)S(1)}, bf16[24,24,128]{2,1,0:T(8,128)(2,1)}, u32[]{:S(2)}) copy-start(bf16[24,24,128]{2,1,0:T(8,128)(2,1)} %copy-done.11) | copy-start | bytes 442372
  288.4 106.8 %copy-start.24 = (f32[1,64,128]{2,1,0:T(8,128)S(1)}, f32[1,64,128]{2,1,0:T(8,128)}, u32[]{:S(2)}) copy-start(f32[1,64,128]{2,1,0:T(8,128)} %convolution_bitcast_fusion.18) | copy-start | bytes 98308
  288.7 107.2 %copy-start.17 = (f32[9,128,64]{1,2,0:T(8,128)S(1)}, f32[9,128,64]{1,2,0:T(8,128)}, u32[]{:S(2)}) copy-start(f32[9,128,64]{1,2,0:T(8,128)} %fusion.17) | copy-start | bytes 884740
  388.0 9.4 %collective-permute-start.13 = (bf16[2,24,64]{2,1,0:T(8,128)(2,1)S(1)}, bf16[2,24,64]{2,1,0:T(8,128)(2,1)S(1)}, u32[]{:S(2)}, u32[]{:S(2)}) collective-permute-start(bf16[2,24,64]{2,1,0:T(8,128)(2,1)S(1)} %bitcast.448), channel_id=1, source_target_pairs={{16,0},{32,16},{48,32},{64,48},{80,64},{96,80},{112,96},{128,112},... | collective-permute-start | bytes 18440 | tf_op jit(solution)/shard_map/ppermute | solution.py:18
  389.3 8.1 collective-permute-start.12
  397.5 12.1 %collective-permute-start.14 = (bf16[28,2,64]{2,1,0:T(2,128)(2,1)S(1)}, bf16[28,2,64]{2,1,0:T(2,128)(2,1)S(1)}, u32[]{:S(2)}, u32[]{:S(2)}) collective-permute-start(bf16[28,2,64]{2,1,0:T(2,128)(2,1)S(1)} %get-tuple-element.40), channel_id=1, source_target_pairs={{1,0},{2,1},{3,2},{4,3},{5,4},{6,5},{7,6},{8,7},{9,8},{10,9},{11,1... | collective-permute-start | bytes 21512 | tf_op jit(solution)/shard_map/ppermute | solution.py:18
  400.1 10.7 %collective-permute-start.15 = (bf16[28,2,64]{2,1,0:T(2,128)(2,1)S(1)}, bf16[28,2,64]{2,1,0:T(2,128)(2,1)S(1)}, u32[]{:S(2)}, u32[]{:S(2)}) collective-permute-start(bf16[28,2,64]{2,1,0:T(2,128)(2,1)S(1)} %get-tuple-element.41), channel_id=1, source_target_pairs={{0,1},{1,2},{2,3},{3,4},{4,5},{5,6},{6,7},{7,8},{8,9},{9,10},{10,1... | collective-permute-start | bytes 21512 | tf_op jit(solution)/shard_map/ppermute | solution.py:17
  (7 other events, 6.9 us)
Sparse Core Ops, SparseCore 0:
  397.5 457.3 all-reduce.2
where the time goes:
time: 869 us; the launch traced here: 865 us
  waiting for transfers between devices  544 us (63%)
  starting transfers between devices  141 us (16%)
  blocking collectives  104 us (12%)
  local copies, waits for them, and re-layouts  32.7 us (4%)
  matrix products  18.6 us (2%)
  between operations  15.1 us (2%)
  other arithmetic  9.2 us (1%)
    psum x1, waiting for transfers between devices, local(): lax.psum((conv_both, bias_both, proj_both), ('segment', 'row', 'col'))  442 us
    psum x1, blocking collectives, local(): lax.psum((conv_both, bias_both, proj_both), ('segment', 'row', 'col'))  98.7 us
    all_to_all x6, starting transfers between devices, mirror(): lax.all_to_all(groups, 'col', split_axis=2, concat_axis=2, tiled=True)  57.7 us
    all_to_all x6, waiting for transfers between devices, mirror(): lax.all_to_all(groups, 'col', split_axis=2, concat_axis=2, tiled=True)  55.8 us
    ppermute x8, starting transfers between devices, extended(): before = lax.ppermute(last, axis, up)  45.1 us
    unnamed x84, local copies, waits for them, and re-layouts  28.4 us
    all_to_all x3, starting transfers between devices, mirror(): lax.all_to_all(groups, 'row', split_axis=2, concat_axis=2, tiled=True)  24.6 us
    ppermute x8, waiting for transfers between devices, extended(): after = lax.ppermute(first, axis, down)  24.4 us
  transfers between devices with their start and end apart: 26, of which 17 were waited for; matrix products, arithmetic and copies ran while one was open for 4% of the time, Pallas kernels for 0%

commit v1 on v0

v1 whole, which is shorter than its diff:
```python
import functools

import numpy as np

import jax
import jax.numpy as jnp
from jax import lax
from jax.experimental import pallas as pl
from jax.experimental.pallas import tpu as pltpu
from jax.sharding import PartitionSpec as P

MESH = pl.DeviceIdType.MESH
F32 = jnp.float32
BF16 = jnp.bfloat16

SIDE = 24
AREA = SIDE * SIDE
C = 128
K = 64
D0 = 2
D1 = 8
WIDE = 40
CONV_ROWS = 9 * C
PROJ_ROW = CONV_ROWS
BIAS_ROW = CONV_ROWS + K
PACK_ROWS = CONV_ROWS + K + 16
GRAD_BLOCKS = 12
GRAD_ROWS = GRAD_BLOCKS * K
DIRECTIONS = ((-1, 0), (1, 0), (0, -1), (0, 1), (-1, -1), (-1, 1), (1, -1), (1, 1))
OPPOSITE = (1, 0, 3, 2, 7, 6, 5, 4)
NT = (((1,), (1,)), ((), ()))
TN = (((0,), (0,)), ((), ()))


def dot(a, b, dims=(((1,), (0,)), ((), ()))):
    return lax.dot_general(a, b, dims, preferred_element_type=F32)


def kernel(
    n,
    factor,
    act,
    cot,
    conv_w,
    bias_w,
    proj_w,
    out_grad,
    out_conv,
    out_bias,
    out_proj,
    weights,
    rolled,
    w0t,
    w1cat,
    back1,
    back0,
    proj_diag,
    proj_twice,
    own_f,
    turned_f,
    stage_f,
    act_t,
    cot_t,
    act_m,
    cot_m,
    send_e0,
    send_c0,
    recv_e0,
    recv_c0,
    hidden1,
    hid_e,
    hid_c,
    recv_e1,
    recv_c1,
    gp1,
    gp1_e,
    gp1_c,
    recv_e2,
    recv_c2,
    gp0,
    gp0_e,
    gp0_c,
    recv_e3,
    recv_c3,
    pad_a,
    pad_b,
    pad_8,
    cols_a,
    cols_b,
    cols_8,
    cols_g,
    pre0,
    bottle0,
    grad_bot,
    bottle1,
    branch1,
    branch0,
    grads,
    grads_send,
    grads_recv,
    acc_send,
    plane_recv,
    line_recv,
    total_recv,
    halo_send,
    halo_recv,
    pair_send,
    pair_recv,
    plane_send_sem,
    plane_recv_sem,
    line_send_sem,
    line_recv_sem,
    all_send_sem,
    all_recv_sem,
):
    seg = lax.axis_index("segment")
    row = lax.axis_index("row")
    col = lax.axis_index("col")
    part = int(round(n**0.5))
    piece = GRAD_ROWS // n
    row_hi, row_lo = row // part, row % part
    col_hi, col_lo = col // part, col % part
    plane_me = row_lo * part + col_lo
    line_me = row_hi * part + col_hi
    off_diagonal = row != col

    def plane_peer(index):
        return (seg, row_hi * part + index // part, col_hi * part + index % part)

    def line_peer(index):
        return (seg, (index // part) * part + row_lo, (index % part) * part + col_lo)

    def neighbour(k):
        dr, dc = DIRECTIONS[k]
        r, c = row + dr, col + dc
        exists = None
        if dr:
            exists = (r >= 0) if dr < 0 else (r < n)
        if dc:
            side = (c >= 0) if dc < 0 else (c < n)
            exists = side if exists is None else jnp.logical_and(exists, side)
        return exists, (seg, r, c)

    for ref in (recv_e0, recv_c0, recv_e1, recv_c1, recv_e2, recv_c2, recv_e3, recv_c3):
        ref[...] = jnp.zeros_like(ref)

    barrier = pltpu.get_barrier_semaphore()

    def signal(device):
        pl.semaphore_signal(barrier, inc=1, device_id=device, device_id_type=MESH)

    greeted = jnp.int32(1 + 2 * (n - 1))
    for k in range(8):
        exists, device = neighbour(k)
        pl.when(exists)(functools.partial(signal, device))
        greeted = greeted + exists.astype(jnp.int32)
    mirror = (seg, col, row)
    pl.when(off_diagonal)(functools.partial(signal, mirror))
    greeted = greeted + off_diagonal.astype(jnp.int32)
    sibling = (1 - seg, row, col)
    signal(sibling)

    @pl.loop(1, n)
    def _(step):
        signal(plane_peer((plane_me + step) % n))
        signal(line_peer((line_me + step) % n))

    weights[seg] = jnp.zeros((PACK_ROWS, 128), BF16)
    weights[seg, 0:CONV_ROWS, 0:K] = conv_w[...]
    weights[seg, PROJ_ROW : PROJ_ROW + K] = proj_w[...]
    bias_row = bias_w[...].astype(F32)
    weights[seg, BIAS_ROW : BIAS_ROW + 16] = jnp.broadcast_to(
        jnp.concatenate([bias_row, bias_row], axis=1), (16, 2 * K)
    ).astype(BF16)

    def turn(flat, out):
        @pl.loop(0, SIDE // 2)
        def _(i):
            two = jnp.concatenate(
                [flat[pl.ds(2 * i, SIDE, stride=SIDE), :], flat[pl.ds(2 * i + 1, SIDE, stride=SIDE), :]], axis=0
            )
            out[pl.ds(pl.multiple_of(i * 2 * SIDE, 16), 2 * SIDE), :] = two.astype(BF16)

    own_f[...] = cot[...].astype(F32)
    turn(own_f, cot_t)
    own_f[...] = act[...].astype(F32)
    turn(own_f, act_t)

    pl.semaphore_wait(barrier, greeted)

    def mirror_copy(src, dst, index):
        return pltpu.make_async_remote_copy(
            src_ref=src,
            dst_ref=dst,
            send_sem=pair_send.at[index],
            recv_sem=pair_recv.at[index],
            device_id=mirror,
            device_id_type=MESH,
        )

    def mirror_start(src, dst, index):
        @pl.when(off_diagonal)
        def _():
            mirror_copy(src, dst, index).start()

        @pl.when(jnp.logical_not(off_diagonal))
        def _():
            dst[...] = src[...]

    def mirror_wait(src, dst, index):
        @pl.when(off_diagonal)
        def _():
            mirror_copy(src, dst, index).wait_recv()

    def sibling_copy(src, dst, index):
        return pltpu.make_async_remote_copy(
            src_ref=src,
            dst_ref=dst,
            send_sem=pair_send.at[index],
            recv_sem=pair_recv.at[index],
            device_id=sibling,
            device_id_type=MESH,
        )

    mirror_start(act_t, act_m, 0)
    weights_copy = sibling_copy(weights.at[seg], weights.at[seg], 2)
    weights_copy.start()

    def halo_copy(phase, k, sources, edges, corners):
        opposite = OPPOSITE[k]
        target = edges.at[opposite] if k < 4 else corners.at[opposite - 4]
        return pltpu.make_async_remote_copy(
            src_ref=sources[k],
            dst_ref=target,
            send_sem=halo_send.at[phase, k],
            recv_sem=halo_recv.at[phase, opposite],
            device_id=neighbour(k)[1],
            device_id_type=MESH,
        )

    def halo_arrival(phase, k, sources, edges, corners):
        target = edges.at[k] if k < 4 else corners.at[k - 4]
        return pltpu.make_async_remote_copy(
            src_ref=target,
            dst_ref=target,
            send_sem=halo_send.at[phase, k],
            recv_sem=halo_recv.at[phase, k],
            device_id=neighbour(k)[1],
            device_id_type=MESH,
        )

    def halo_start(phase, sources, edges, corners):
        for k in (7, 6, 5, 4, 3, 2, 1, 0):
            pl.when(neighbour(k)[0])(
                lambda k=k: halo_copy(phase, k, sources, edges, corners).start()
            )

    def halo_wait(phase, sources, edges, corners):
        for k in range(8):
            pl.when(neighbour(k)[0])(
                lambda k=k: halo_arrival(phase, k, sources, edges, corners).wait_recv()
            )

    def halo_sent(phase, sources, edges, corners):
        for k in range(8):
            pl.when(neighbour(k)[0])(
                lambda k=k: halo_copy(phase, k, sources, edges, corners).wait_send()
            )

    def pack_narrow(tiles, edges, corners):
        strip = D0 * SIDE
        for t, tile in enumerate(tiles):
            at = slice(t * strip, (t + 1) * strip)
            edges[0, at] = tile[0:strip].astype(BF16)
            edges[1, at] = tile[AREA - strip : AREA].astype(BF16)
            for k, first in ((2, 0), (3, SIDE - D0)):
                columns = [tile[pl.ds(first + j, SIDE, stride=SIDE), :] for j in range(D0)]
                edges[k, at] = jnp.concatenate(columns, axis=0).astype(BF16)
        for k, (r, c) in enumerate(((0, 0), (0, SIDE - D0), (SIDE - D0, 0), (SIDE - D0, SIDE - D0))):
            stage_f[0:16] = jnp.zeros((16, C), F32)
            for t, tile in enumerate(tiles):
                for i in range(D0):
                    start = (r + i) * SIDE + c
                    stage_f[t * 4 + i * D0 : t * 4 + (i + 1) * D0] = tile[start : start + D0]
            corners[k] = stage_f[0:16].astype(BF16)

    def unpack_narrow(t, edges, corners, pad, change):
        strip = D0 * SIDE
        at = slice(t * strip, (t + 1) * strip)
        north = change(edges[0, at].astype(F32))
        south = change(edges[1, at].astype(F32))
        west = change(edges[2, at].astype(F32))
        east = change(edges[3, at].astype(F32))
        for i in range(D0):
            lines = slice(i * SIDE, (i + 1) * SIDE)
            pad[i * WIDE + 8 : i * WIDE + 8 + SIDE] = north[lines]
            low = (D0 + SIDE + i) * WIDE + 8
            pad[low : low + SIDE] = south[lines]
            pad[pl.ds(D0 * WIDE + 8 - D0 + i, SIDE, stride=WIDE), :] = west[lines]
            pad[pl.ds(D0 * WIDE + 8 + SIDE + i, SIDE, stride=WIDE), :] = east[lines]
        for k, (r, c) in enumerate(((0, 8 - D0), (0, 8 + SIDE), (D0 + SIDE, 8 - D0), (D0 + SIDE, 8 + SIDE))):
            stage_f[0:16] = change(corners[k].astype(F32))
            for i in range(D0):
                start = (r + i) * WIDE + c
                pad[start : start + D0] = stage_f[t * 4 + i * D0 : t * 4 + (i + 1) * D0]

    def fill_centre(tile, pad, dilation, change):
        for i in range(SIDE):
            start = (dilation + i) * WIDE + 8
            pad[start : start + SIDE] = change(tile[i * SIDE : (i + 1) * SIDE])

    def pack_wide(tile, edges, corners):
        for k, first in ((0, 0), (1, SIDE - D1)):
            edges[k] = jnp.concatenate(
                [tile[i * SIDE + first : i * SIDE + first + D1] for i in range(SIDE)], axis=0
            ).astype(BF16)
        for k, (r, c) in enumerate(((0, 0), (0, SIDE - D1), (SIDE - D1, 0), (SIDE - D1, SIDE - D1))):
            corners[k] = jnp.concatenate(
                [tile[(r + i) * SIDE + c : (r + i) * SIDE + c + D1] for i in range(D1)], axis=0
            ).astype(BF16)

    def wide_sources(flat, edges, corners):
        strip = D1 * SIDE
        return (
            flat.at[0:strip],
            flat.at[AREA - strip : AREA],
            edges.at[0],
            edges.at[1],
        ) + tuple(corners.at[k] for k in range(4))

    def unpack_wide(edges, corners, pad):
        north = edges[0].astype(F32)
        south = edges[1].astype(F32)
        west = edges[2].astype(F32)
        east = edges[3].astype(F32)
        for i in range(D1):
            lines = slice(i * SIDE, (i + 1) * SIDE)
            pad[i * WIDE + D1 : i * WIDE + D1 + SIDE] = north[lines]
            low = (D1 + SIDE + i) * WIDE + D1
            pad[low : low + SIDE] = south[lines]
        for i in range(SIDE):
            lines = slice(i * D1, (i + 1) * D1)
            start = (D1 + i) * WIDE
            pad[start : start + D1] = west[lines]
            pad[start + D1 + SIDE : start + WIDE] = east[lines]
        for k, (r, c) in enumerate(((0, 0), (0, D1 + SIDE), (D1 + SIDE, 0), (D1 + SIDE, D1 + SIDE))):
            corner = corners[k].astype(F32)
            for i in range(D1):
                start = (r + i) * WIDE + c
                pad[start : start + D1] = corner[i * D1 : (i + 1) * D1]

    def spread(pad, cols, dilation):
        for b in range(3):
            first = 8 + (b - 1) * dilation
            for i in range(0, SIDE + 2 * dilation, 2):
                two = jnp.concatenate(
                    [pad[(i + h) * WIDE + first : (i + h) * WIDE + first + SIDE] for h in range(2)], axis=0
                )
                cols[i * SIDE : (i + 2) * SIDE, b * C : (b + 1) * C] = two.astype(BF16)

    same = lambda x: x
    relu = lambda x: jnp.maximum(x, 0.0)

    fill_centre(own_f, pad_a, D0, relu)
    weights_copy.wait_recv()
    for s in range(2):
        rolled[s] = pltpu.roll(weights[s, 0:CONV_ROWS].astype(F32), K, 1).astype(BF16)
    proj_diag[...] = jnp.zeros_like(proj_diag)
    proj_diag[0:K, 0:C] = weights[0, PROJ_ROW : PROJ_ROW + K]
    proj_diag[K : 2 * K, C : 2 * C] = weights[0, PROJ_ROW : PROJ_ROW + K]
    for s in range(2):
        for h in range(2):
            proj_twice[s, h * K : (h + 1) * K] = weights[s, PROJ_ROW : PROJ_ROW + K]
    tap = lambda a, b: slice((3 * a + b) * C, (3 * a + b + 1) * C)
    for a in range(3):
        for b in range(3):
            w0t[tap(a, b)] = rolled[0, tap(b, a)]
            w1cat[tap(a, b)] = weights[1, tap(a, b)] + rolled[1, tap(b, a)]
            lanes = slice(b * C, (b + 1) * C)
            back0[a, :, lanes] = weights[0, tap(2 - a, 2 - b)]
            back1[a, 0:C, lanes] = weights[1, tap(2 - a, 2 - b)]
            back1[a, C : 2 * C, lanes] = rolled[1, tap(2 - b, 2 - a)]

    mirror_wait(act_t, act_m, 0)
    turned_f[...] = act_m[...].astype(F32)
    pack_narrow((own_f, turned_f), send_e0, send_c0)
    sources0 = tuple(send_e0.at[k] for k in range(4)) + tuple(send_c0.at[k] for k in range(4))
    halo0 = (0, sources0, recv_e0, recv_c0)
    halo_start(*halo0)
    mirror_start(cot_t, cot_m, 1)
    fill_centre(turned_f, pad_b, D0, relu)
    halo_wait(*halo0)
    unpack_narrow(0, recv_e0, recv_c0, pad_a, relu)
    unpack_narrow(1, recv_e0, recv_c0, pad_b, relu)
    spread(pad_a, cols_a, D0)
    spread(pad_b, cols_b, D0)

    chunk = 192
    shift0 = D0 * SIDE
    shift1 = D1 * SIDE
    wide = 3 * C

    def rows_at(base, extra=0):
        return pl.ds(pl.multiple_of(base + extra, 16), chunk)

    bias0 = weights[0, BIAS_ROW : BIAS_ROW + 16].astype(F32)[0:1]
    bias1 = weights[1, BIAS_ROW : BIAS_ROW + 16].astype(F32)[0:1]

    @pl.loop(0, AREA // chunk)
    def _(i):
        base = i * chunk
        total = bias0
        for a in range(3):
            total = total + dot(cols_a[rows_at(base, a * shift0), :], weights[0, a * wide : (a + 1) * wide])
        for a in range(3):
            total = total + dot(cols_b[rows_at(base, a * shift0), :], w0t[a * wide : (a + 1) * wide])
        pre0[rows_at(base), :] = total
        bottle = jnp.maximum(total, 0.0).astype(BF16)
        bottle0[rows_at(base), :] = bottle
        both = dot(bottle, proj_diag[...])
        own = (own_f[rows_at(base), :] + both[:, 0:C]).astype(BF16).astype(F32)
        turned = (turned_f[rows_at(base), :] + both[:, C : 2 * C]).astype(BF16).astype(F32)
        sym = ((own + turned) * 0.5).astype(BF16)
        hidden1[rows_at(base), :] = jnp.maximum(sym, jnp.zeros_like(sym))

    turned_f[...] = hidden1[...].astype(F32)
    pack_wide(turned_f, hid_e, hid_c)
    halo1 = (1, wide_sources(hidden1, hid_e, hid_c), recv_e1, recv_c1)
    halo_start(*halo1)
    fill_centre(turned_f, pad_8, D1, same)
    mirror_wait(cot_t, cot_m, 1)

    @pl.loop(0, AREA // chunk)
    def _(i):
        at = rows_at(i * chunk)
        branch = ((cot[at, :].astype(F32) + cot_m[at, :].astype(F32)) * 0.5).astype(BF16)
        branch1[at, :] = branch
        grad_bot[at, :] = dot(branch, proj_twice[1], NT)

    halo_wait(*halo1)
    unpack_wide(recv_e1, recv_c1, pad_8)
    spread(pad_8, cols_8, D1)

    @pl.loop(0, AREA // chunk)
    def _(i):
        base = i * chunk
        total = bias1
        for a in range(3):
            total = total + dot(cols_8[rows_at(base, a * shift1), :], w1cat[a * wide : (a + 1) * wide])
        bottle1[rows_at(base), :] = jnp.maximum(total, 0.0).astype(BF16)
        grad = jnp.where(total > 0, grad_bot[rows_at(base), :], 0.0)
        turned_f[rows_at(base), :] = grad
        gp1[rows_at(base), :] = grad.astype(BF16)

    pack_wide(turned_f, gp1_e, gp1_c)
    halo2 = (2, wide_sources(gp1, gp1_e, gp1_c), recv_e2, recv_c2)
    halo_start(*halo2)
    fill_centre(turned_f, pad_8, D1, lambda x: x)

    ones = jnp.ones((AREA, C), BF16)

    def weight_gradients(s, grad_pre, cols, shift, bottle, branch):
        for a in range(3):
            product = dot(grad_pre[...], cols[a * shift : a * shift + AREA, :], TN)
            for b in range(3):
                at = (3 * a + b) * K
                grads[s, at : at + K] = product[0:K, b * C : (b + 1) * C].astype(BF16)
        grads[s, 9 * K : 10 * K] = dot(bottle[...], branch[...], TN)[0:K].astype(BF16)
        grads[s, 10 * K : 11 * K] = dot(grad_pre[...], ones, TN)[0:K].astype(BF16)
        grads[s, 11 * K : 12 * K] = jnp.zeros((K, C), BF16)

    weight_gradients(1, gp1, cols_8, shift1, bottle1, branch1)
    halo_wait(*halo2)
    unpack_wide(recv_e2, recv_c2, pad_8)
    spread(pad_8, cols_g, D1)

    @pl.loop(0, AREA // chunk)
    def _(i):
        base = i * chunk
        total = None
        for a in range(3):
            term = dot(cols_g[rows_at(base, a * shift1), :], back1[a], NT)
            total = term if total is None else total + term
        branch = branch1[rows_at(base), :].astype(F32)
        live = hidden1[rows_at(base), :].astype(F32) > 0
        own = (branch + jnp.where(live, total[:, 0:C], 0.0)).astype(BF16).astype(F32)
        turned = (branch + jnp.where(live, total[:, C : 2 * C], 0.0)).astype(BF16).astype(F32)
        mean = ((own + turned) * 0.5).astype(BF16)
        branch0[rows_at(base), :] = mean
        grad = jnp.where(pre0[rows_at(base), :] > 0, dot(mean, proj_twice[0], NT), 0.0)
        turned_f[rows_at(base), :] = grad
        gp0[rows_at(base), :] = grad.astype(BF16)

    pack_narrow((turned_f,), gp0_e, gp0_c)
    sources3 = tuple(gp0_e.at[k] for k in range(4)) + tuple(gp0_c.at[k] for k in range(4))
    halo3 = (3, sources3, recv_e3, recv_c3)
    halo_start(*halo3)
    weight_gradients(0, gp0, cols_a, shift0, bottle0, branch0)

    grads_copy = sibling_copy(grads.at[1 - seg], grads_recv, 3)
    grads_copy.start()
    fill_centre(turned_f, pad_a, D0, same)
    grads_copy.wait_recv()
    acc_send[...] = (grads[seg].astype(F32) + grads_recv[...].astype(F32)).astype(BF16)

    def piece_at(index):
        return pl.ds(pl.multiple_of(index * piece, 16), piece)

    def group_copy(step, me, peer, src, dst, send_sem, recv_sem, index):
        return pltpu.make_async_remote_copy(
            src_ref=src,
            dst_ref=dst.at[index],
            send_sem=send_sem.at[step],
            recv_sem=recv_sem.at[index],
            device_id=peer,
            device_id_type=MESH,
        )

    def plane_copy(step):
        to = (plane_me + step) % n
        return group_copy(
            step, plane_me, plane_peer(to), acc_send.at[piece_at(to)], plane_recv, plane_send_sem, plane_recv_sem, plane_me
        )

    def line_copy(step):
        to = (line_me + step) % n
        return group_copy(
            step, line_me, line_peer(to), line_recv.at[line_me], line_recv, line_send_sem, line_recv_sem, line_me
        )

    def all_copy(step):
        to = (plane_me + step) % n
        return group_copy(
            step, plane_me, plane_peer(to), total_recv.at[plane_me], total_recv, all_send_sem, all_recv_sem, plane_me
        )

    def arrivals(me, peer, dst, send_sem, recv_sem):
        @pl.loop(1, n)
        def _(step):
            index = (me + step) % n
            group_copy(step, me, peer(index), dst.at[index], dst, send_sem, recv_sem, index).wait_recv()

    def add_up(buffer):
        total = buffer[0].astype(F32)
        for i in range(1, n):
            total = total + buffer[i].astype(F32)
        return total

    pl.loop(1, n)(lambda step: plane_copy(step).start())
    plane_recv[plane_me] = acc_send[piece_at(plane_me), :]

    halo_wait(*halo3)
    unpack_narrow(0, recv_e3, recv_c3, pad_a, same)
    spread(pad_a, cols_b, D0)

    @pl.loop(0, AREA // chunk)
    def _(i):
        base = i * chunk
        total = None
        for a in range(3):
            term = dot(cols_b[rows_at(base, a * shift0), :], back0[a], NT)
            total = term if total is None else total + term
        branch = branch0[rows_at(base), :].astype(F32)
        live = own_f[rows_at(base), :] > 0
        out_grad[rows_at(base), :] = (branch + jnp.where(live, total, 0.0)).astype(BF16)

    arrivals(plane_me, plane_peer, plane_recv, plane_send_sem, plane_recv_sem)
    line_recv[line_me] = add_up(plane_recv).astype(BF16)
    pl.loop(1, n)(lambda step: line_copy(step).start())
    arrivals(line_me, line_peer, line_recv, line_send_sem, line_recv_sem)
    total_recv[plane_me] = add_up(line_recv).astype(BF16)
    pl.loop(1, n)(lambda step: all_copy(step).start())

    pl.when(off_diagonal)(lambda: mirror_copy(act_t, act_m, 0).wait_send())
    pl.when(off_diagonal)(lambda: mirror_copy(cot_t, cot_m, 1).wait_send())
    weights_copy.wait_send()
    grads_copy.wait_send()
    for halo in (halo0, halo1, halo2, halo3):
        halo_sent(*halo)
    pl.loop(1, n)(lambda step: plane_copy(step).wait_send())
    pl.loop(1, n)(lambda step: line_copy(step).wait_send())

    arrivals(plane_me, plane_peer, total_recv, all_send_sem, all_recv_sem)
    for i in range(n):
        stage_f[i * piece : (i + 1) * piece] = total_recv[i].astype(F32) * factor
    for t in range(9):
        out_conv[t * C : (t + 1) * C] = stage_f[t * K : (t + 1) * K].T
    out_proj[...] = stage_f[9 * K : 10 * K]
    out_bias[...] = stage_f[10 * K : 11 * K].T[0:8]
    pl.loop(1, n)(lambda step: all_copy(step).wait_send())


def solution(mesh):
    n = mesh.shape["row"]
    cells = mesh.shape["segment"] * (SIDE * n) * (SIDE * n)
    factor = float(np.float32(1.0) / np.sqrt(np.float32(cells)))
    piece = GRAD_ROWS // n
    vmem = pltpu.VMEM
    scratch = [
        vmem((2, PACK_ROWS, 128), BF16),
        vmem((2, CONV_ROWS, 128), BF16),
        vmem((CONV_ROWS, 128), BF16),
        vmem((CONV_ROWS, 128), BF16),
        vmem((3, 2 * C, 3 * C), BF16),
        vmem((3, C, 3 * C), BF16),
        vmem((2 * K, 2 * C), BF16),
        vmem((2, 2 * K, C), BF16),
        vmem((AREA, C), F32),
        vmem((AREA, C), F32),
        vmem((GRAD_ROWS, C), F32),
        vmem((AREA, C), BF16),
        vmem((AREA, C), BF16),
        vmem((AREA, C), BF16),
        vmem((AREA, C), BF16),
        vmem((4, 2 * D0 * SIDE, C), BF16),
        vmem((4, 16, C), BF16),
        vmem((4, 2 * D0 * SIDE, C), BF16),
        vmem((4, 16, C), BF16),
        vmem((AREA, C), BF16),
        vmem((2, D1 * SIDE, C), BF16),
        vmem((4, D1 * D1, C), BF16),
        vmem((4, D1 * SIDE, C), BF16),
        vmem((4, D1 * D1, C), BF16),
        vmem((AREA, C), BF16),
        vmem((2, D1 * SIDE, C), BF16),
        vmem((4, D1 * D1, C), BF16),
        vmem((4, D1 * SIDE, C), BF16),
        vmem((4, D1 * D1, C), BF16),
        vmem((AREA, C), BF16),
        vmem((4, D0 * SIDE, C), BF16),
        vmem((4, 16, C), BF16),
        vmem((4, D0 * SIDE, C), BF16),
        vmem((4, 16, C), BF16),
        vmem(((SIDE + 2 * D0) * WIDE, C), F32),
        vmem(((SIDE + 2 * D0) * WIDE, C), F32),
        vmem(((SIDE + 2 * D1) * WIDE, C), F32),
        vmem(((SIDE + 2 * D0) * SIDE, 3 * C), BF16),
        vmem(((SIDE + 2 * D0) * SIDE, 3 * C), BF16),
        vmem(((SIDE + 2 * D1) * SIDE, 3 * C), BF16),
        vmem(((SIDE + 2 * D1) * SIDE, 3 * C), BF16),
        vmem((AREA, C), F32),
        vmem((AREA, C), BF16),
        vmem((AREA, C), F32),
        vmem((AREA, C), BF16),
        vmem((AREA, C), BF16),
        vmem((AREA, C), BF16),
        vmem((2, GRAD_ROWS, C), BF16),
        vmem((16, C), BF16),
        vmem((GRAD_ROWS, C), BF16),
        vmem((GRAD_ROWS, C), BF16),
        vmem((n, piece, C), BF16),
        vmem((n, piece, C), BF16),
        vmem((n, piece, C), BF16),
        pltpu.SemaphoreType.DMA((4, 8)),
        pltpu.SemaphoreType.DMA((4, 8)),
        pltpu.SemaphoreType.DMA((4,)),
        pltpu.SemaphoreType.DMA((4,)),
    ] + [pltpu.SemaphoreType.DMA((n,))] * 6

    call = pl.pallas_call(
        functools.partial(kernel, n, factor),
        out_shape=(
            jax.ShapeDtypeStruct((AREA, C), BF16),
            jax.ShapeDtypeStruct((CONV_ROWS, K), F32),
            jax.ShapeDtypeStruct((8, K), F32),
            jax.ShapeDtypeStruct((K, C), F32),
        ),
        in_specs=[pl.BlockSpec(memory_space=pltpu.VMEM)] * 5,
        out_specs=[pl.BlockSpec(memory_space=pltpu.VMEM)] * 4,
        scratch_shapes=scratch,
        compiler_params=pltpu.CompilerParams(
            collective_id=0, has_side_effects=True, vmem_limit_bytes=40 * 1024 * 1024
        ),
        name="trunk",
    )

    def local(activations, cotangent, conv_weight, conv_bias, out_weight):
        grad, conv, bias, proj = call(
            activations.reshape(AREA, C),
            cotangent.reshape(AREA, C),
            conv_weight.reshape(CONV_ROWS, K),
            conv_bias,
            out_weight.reshape(K, C),
        )
        return (
            grad.reshape(1, SIDE, SIDE, C),
            conv.reshape(1, 9, C, K),
            bias[0:1],
            proj.reshape(1, K, C),
        )

    in_specs = (
        P("segment", "row", "col", None),
        P("segment", "row", "col", None),
        P("segment", None, None, None),
        P("segment", None),
        P("segment", None, None),
    )
    out_specs = (
        P("segment", "row", "col", None),
        P("segment", None, None, None),
        P("segment", None),
        P("segment", None, None),
    )
    return jax.shard_map(local, mesh=mesh, in_specs=in_specs, out_specs=out_specs, check_vma=False)
```

time: 869 us -> 100 us (0.12)
  waiting for transfers between devices: 544 us -> 0 us
  starting transfers between devices: 141 us -> 0 us
  blocking collectives: 104 us -> 0 us
  Pallas kernels: 0 us -> 93 us
  local copies, waits for them, and re-layouts: 32.7 us -> 4.53 us
  matrix products: 18.6 us -> 0 us
  between operations: 15.1 us -> 0.7 us
  other arithmetic: 9.2 us -> 0 us
    psum x1 -> x0, waiting for transfers between devices: 442 us -> none  [local(): lax.psum((conv_both, bias_both, proj_both), ('segment', 'row', 'col'))]
    psum x1 -> x0, blocking collectives: 98.7 us -> none  [local(): lax.psum((conv_both, bias_both, proj_both), ('segment', 'row', 'col'))]
    pallas_call x0 -> x1, Pallas kernels: none -> 93 us  [local(): call(activations.reshape(AREA, C), cotangent.reshape(AREA, C), conv_weigh...]
    all_to_all x9 -> x0, starting transfers between devices: 82.3 us -> none  [the longest x6 57.7 us: mirror(): lax.all_to_all(groups, 'col', split_axis=2, concat_axis=2, tiled=True)]
    all_to_all x9 -> x0, waiting for transfers between devices: 74.5 us -> none  [the longest x6 55.8 us: mirror(): lax.all_to_all(groups, 'col', split_axis=2, concat_axis=2, tiled=True)]
    ppermute x16 -> x0, starting transfers between devices: 58.9 us -> none  [the longest x8 45.1 us: extended(): before = lax.ppermute(last, axis, up)]
    ppermute x16 -> x0, waiting for transfers between devices: 27.3 us -> none  [the longest x8 24.4 us: extended(): after = lax.ppermute(first, axis, down)]
    unnamed x84 -> x12, local copies, waits for them, and re-layouts: 28.4 us -> 4.01 us
  transfers between devices with their start and end apart: 26 -> 0, of which waited for: 17 -> 0; matrix products, arithmetic and copies ran while one was open for 4% -> 0% of each run, Pallas kernels for 0% -> 0%
where the time goes in v1:
time: 100 us; the launch traced here: 98.2 us
  Pallas kernels  93 us (93%)
  local copies, waits for them, and re-layouts  4.53 us (5%)
    pallas_call x1, Pallas kernels, local(): call(activations.reshape(AREA, C), cotangent.reshape(AREA, C), conv_weigh...  93 us
    unnamed x12, local copies, waits for them, and re-layouts  4.01 us

profile of v1, /device:TPU:6, one launch (start us, length us, event | category | flops | bytes accessed | tf_op | source)
XLA Modules:
  0.0 98.2 jit_solution(16047337129785729486)
XLA Ops:
  0.6 0.0 copy-start
  0.6 0.0 copy-start.1
  0.7 0.0 copy-start.2
  0.7 1.2 %copy.9 = bf16[1,9,128,64]{3,2,1,0:T(8,128)(2,1)S(1)} copy(bf16[1,9,128,64]{2,3,1,0:T(8,128)(2,1)} %param.7) | data formatting | bytes 294912 | tf_op args[2]
  1.8 0.0 copy-start.3
  1.8 0.0 copy-done
  1.9 0.0 copy-done.1
  1.9 0.0 copy-done.2
  1.9 0.6 copy-done.3
  2.5 93.0 %trunk.1 = (bf16[576,128]{1,0:T(8,128)(2,1)S(1)}, f32[1152,64]{1,0:T(8,128)S(1)}, f32[8,64]{1,0:T(8,128)S(1)}, f32[64,128]{1,0:T(8,128)S(1)}) custom-call(bf16[576,128]{1,0:T(8,128)(2,1)S(1)} %bitcast.10, bf16[576,128]{1,0:T(8,128)(2,1)S(1)} %bitcast.11, bf16[1152,64]{1,0:T(8,128)(2,1)S(1)} %bitcast.7, bf16[1,64]{1,0:T(2,128)(2,1)S(1)} %copy-done.3, ...), custom_call_target="tpu_custom_call" | custom-call | tf_op jit(solution)/shard_map/trunk/pallas_call | solution.py:678
  95.5 0.9 copy.10
  96.4 0.5 slice.3
  96.9 0.7 copy.13
  97.6 0.6 copy.14
Async XLA Ops:
  0.6 1.2 %copy-start = (bf16[1,24,24,128]{3,2,1,0:T(8,128)(2,1)S(1)}, bf16[1,24,24,128]{3,2,1,0:T(8,128)(2,1)}, u32[]{:S(2)}) copy-start(bf16[1,24,24,128]{3,2,1,0:T(8,128)(2,1)} %param.5) | copy-start | bytes 442372
  0.6 1.2 %copy-start.1 = (bf16[1,24,24,128]{3,2,1,0:T(8,128)(2,1)S(1)}, bf16[1,24,24,128]{3,2,1,0:T(8,128)(2,1)}, u32[]{:S(2)}) copy-start(bf16[1,24,24,128]{3,2,1,0:T(8,128)(2,1)} %param.6) | copy-start | bytes 442372
  0.7 1.2 %copy-start.2 = (bf16[1,64,128]{2,1,0:T(8,128)(2,1)S(1)}, bf16[1,64,128]{2,1,0:T(8,128)(2,1)}, u32[]{:S(2)}) copy-start(bf16[1,64,128]{2,1,0:T(8,128)(2,1)} %param.9) | copy-start | bytes 49156
  1.8 0.7 copy-start.3

commit v2 on v1

v2 whole, which is shorter than its diff:
```python
import functools

import numpy as np

import jax
import jax.numpy as jnp
from jax import lax
from jax.experimental import pallas as pl
from jax.experimental.pallas import tpu as pltpu
from jax.sharding import PartitionSpec as P

MESH = pl.DeviceIdType.MESH
F32 = jnp.float32
BF16 = jnp.bfloat16

SIDE = 24
AREA = SIDE * SIDE
C = 128
K = 64
D0 = 2
D1 = 8
WIDE = 40
CONV_ROWS = 9 * K
PROJ_ROW = CONV_ROWS
BIAS_ROW = CONV_ROWS + K
PACK_ROWS = CONV_ROWS + K + 16
GRAD_BLOCKS = 12
GRAD_ROWS = GRAD_BLOCKS * K
DIRECTIONS = ((-1, 0), (1, 0), (0, -1), (0, 1), (-1, -1), (-1, 1), (1, -1), (1, 1))
OPPOSITE = (1, 0, 3, 2, 7, 6, 5, 4)
NT = (((1,), (1,)), ((), ()))
TN = (((0,), (0,)), ((), ()))


def dot(a, b, dims=(((1,), (0,)), ((), ()))):
    return lax.dot_general(a, b, dims, preferred_element_type=F32)


def kernel(
    n,
    factor,
    act_in,
    cot_in,
    conv_in,
    bias_in,
    proj_in,
    out_grad,
    out_conv,
    out_bias,
    out_proj,
    act,
    cot,
    bias_w,
    weights,
    first,
    second,
    back1,
    back0,
    proj_pad,
    proj_twice,
    own_f,
    work_f,
    stage_f,
    sum_t,
    cot_t,
    sum_m,
    cot_m,
    send_e0,
    send_c0,
    recv_e0,
    recv_c0,
    hidden1,
    hid_e,
    hid_c,
    recv_e1,
    recv_c1,
    gp1,
    gp1_e,
    gp1_c,
    recv_e2,
    recv_c2,
    gp0,
    gp0_e,
    gp0_c,
    recv_e3,
    recv_c3,
    pad_a,
    pad_8,
    pad_9,
    cols_a,
    cols_b,
    cols_8,
    cols_g,
    pre0,
    bottle0,
    grad_bot,
    bottle1,
    branch1,
    branch0,
    grads,
    plane_recv,
    line_recv,
    total_recv,
    halo_send,
    halo_recv,
    pair_send,
    pair_recv,
    plane_send_sem,
    plane_recv_sem,
    line_send_sem,
    line_recv_sem,
    all_send_sem,
    all_recv_sem,
    greeting,
    partner,
    input_sem,
):
    seg = lax.axis_index("segment")
    row = lax.axis_index("row")
    col = lax.axis_index("col")
    part = int(round(n**0.5))
    piece = GRAD_ROWS // n
    row_hi, row_lo = row // part, row % part
    col_hi, col_lo = col // part, col % part
    plane_me = row_lo * part + col_lo
    line_me = row_hi * part + col_hi
    off_diagonal = row != col
    mirror = (seg, col, row)
    sibling = (1 - seg, row, col)

    def plane_peer(section, index):
        return (section, row_hi * part + index // part, col_hi * part + index % part)

    def line_peer(index):
        return (seg, (index // part) * part + row_lo, (index % part) * part + col_lo)

    def row_peer(step):
        return (seg, ((row_hi + step) % part) * part + row_lo, col)

    def col_peer(step):
        return (seg, row, ((col_hi + step) % part) * part + col_lo)

    def there(k):
        dr, dc = DIRECTIONS[k]
        r, c = row + dr, col + dc
        exists = None
        if dr:
            exists = (r >= 0) if dr < 0 else (r < n)
        if dc:
            side = (c >= 0) if dc < 0 else (c < n)
            exists = side if exists is None else jnp.logical_and(exists, side)
        return exists

    def neighbour(k):
        dr, dc = DIRECTIONS[k]
        return (seg, row + dr, col + dc)

    inputs = [
        pltpu.make_async_copy(src, dst, input_sem.at[i])
        for i, (src, dst) in enumerate(
            (
                (act_in, act),
                (cot_in, cot),
                (conv_in, weights.at[seg, 0:CONV_ROWS]),
                (proj_in, weights.at[seg, PROJ_ROW : PROJ_ROW + K]),
                (bias_in, bias_w),
            )
        )
    ]
    for copy in inputs:
        copy.start()
    barrier = pltpu.get_barrier_semaphore()

    def signal(device):
        pl.semaphore_signal(barrier, inc=1, device_id=device, device_id_type=MESH)

    greeted = jnp.int32(1 + 2 * (part - 1))
    pl.when(off_diagonal)(functools.partial(signal, mirror))
    greeted = greeted + off_diagonal.astype(jnp.int32)
    for step in range(1, part):
        signal(col_peer(step))
        signal(row_peer(step))
    for k in range(7, -1, -1):
        pl.when(there(k))(functools.partial(signal, neighbour(k)))
        greeted = greeted + there(k).astype(jnp.int32)
    signal(sibling)

    def turn(flat, out):
        @pl.loop(0, SIDE // 2)
        def _(i):
            two = jnp.concatenate(
                [flat[pl.ds(2 * i, SIDE, stride=SIDE), :], flat[pl.ds(2 * i + 1, SIDE, stride=SIDE), :]], axis=0
            )
            out[pl.ds(pl.multiple_of(i * 2 * SIDE, 16), 2 * SIDE), :] = two.astype(BF16)

    strip = D0 * SIDE
    corners_of_tile = ((0, 0), (0, SIDE - D0), (SIDE - D0, 0), (SIDE - D0, SIDE - D0))

    def pack_corners(tile, corners):
        for k, (r, c) in enumerate(corners_of_tile):
            stage_f[...] = jnp.zeros((16, C), F32)
            for i in range(D0):
                start = (r + i) * SIDE + c
                stage_f[i * D0 : (i + 1) * D0] = tile[start : start + D0]
            corners[k] = stage_f[...].astype(BF16)

    def pack_narrow(tile, edges, corners):
        edges[0] = tile[0:strip].astype(BF16)
        edges[1] = tile[AREA - strip : AREA].astype(BF16)
        for k, first_column in ((2, 0), (3, SIDE - D0)):
            columns = [tile[pl.ds(first_column + j, SIDE, stride=SIDE), :] for j in range(D0)]
            edges[k] = jnp.concatenate(columns, axis=0).astype(BF16)
        pack_corners(tile, corners)

    for copy in inputs:
        copy.wait()
    own_f[...] = act[...].astype(F32)
    pack_narrow(own_f, send_e0, send_c0)
    bias_row = bias_w[...].astype(F32)
    weights[seg, BIAS_ROW : BIAS_ROW + 16] = jnp.broadcast_to(
        jnp.concatenate([bias_row, bias_row], axis=1), (16, 2 * K)
    ).astype(BF16)
    work_f[...] = cot[...].astype(F32)
    turn(work_f, cot_t)

    pl.semaphore_wait(barrier, greeted)

    def pair_copy(src, dst, index, device):
        return pltpu.make_async_remote_copy(
            src_ref=src,
            dst_ref=dst,
            send_sem=pair_send.at[index],
            recv_sem=pair_recv.at[index],
            device_id=device,
            device_id_type=MESH,
        )

    def mirror_copy(src, dst, index):
        return pair_copy(src, dst, index, mirror)

    def mirror_start(src, dst, index):
        @pl.when(off_diagonal)
        def _():
            mirror_copy(src, dst, index).start()

        @pl.when(jnp.logical_not(off_diagonal))
        def _():
            dst[...] = src[...]

    def mirror_wait(src, dst, index):
        pl.when(off_diagonal)(lambda: mirror_copy(src, dst, index).wait_recv())

    def halo_to(phase, k, slot, device, sources, edges, corners):
        return pltpu.make_async_remote_copy(
            src_ref=sources[k],
            dst_ref=edges.at[slot] if slot < 4 else corners.at[slot - 4],
            send_sem=halo_send.at[phase, k],
            recv_sem=halo_recv.at[phase, slot],
            device_id=device,
            device_id_type=MESH,
        )

    def halo_copy(phase, k, sources, edges, corners):
        return halo_to(phase, k, OPPOSITE[k], neighbour(k), sources, edges, corners)

    def halo_start(*halo):
        for k in range(7, -1, -1):
            pl.when(there(k))(lambda k=k: halo_copy(halo[0], k, *halo[1:]).start())

    def halo_clear(phase, sources, edges, corners):
        for k in range(8):

            @pl.when(jnp.logical_not(there(k)))
            def _():
                ref = edges.at[k] if k < 4 else corners.at[k - 4]
                ref[...] = jnp.zeros_like(ref)

    def arrived(phase, k, edges, corners):
        target = edges.at[k] if k < 4 else corners.at[k - 4]
        return pltpu.make_async_remote_copy(
            src_ref=target,
            dst_ref=target,
            send_sem=halo_send.at[phase, k],
            recv_sem=halo_recv.at[phase, k],
            device_id=neighbour(k),
            device_id_type=MESH,
        )

    def halo_wait(phase, sources, edges, corners):
        for k in range(8):
            pl.when(there(k))(lambda k=k: arrived(phase, k, edges, corners).wait_recv())

    def halo_sent(*halo):
        for k in range(8):
            pl.when(there(k))(lambda k=k: halo_copy(halo[0], k, *halo[1:]).wait_send())

    sources0 = tuple(send_e0.at[k] for k in range(4)) + tuple(send_c0.at[k] for k in range(4))
    halo0 = (0, sources0, recv_e0, recv_c0)
    halo_start(*halo0)
    weights_copy = pair_copy(weights.at[seg], weights.at[seg], 2, sibling)
    weights_copy.start()
    mirror_start(cot_t, cot_m, 1)
    for step in range(1, part):
        pl.semaphore_signal(greeting, inc=1, device_id=row_peer(step), device_id_type=MESH)

    halo_clear(*halo0)
    halo_clear(1, None, recv_e1, recv_c1)
    halo_clear(2, None, recv_e2, recv_c2)
    halo_clear(3, None, recv_e3, recv_c3)

    def unpack_narrow(edges, corners, pad, change):
        north = change(edges[0].astype(F32))
        south = change(edges[1].astype(F32))
        west = change(edges[2].astype(F32))
        east = change(edges[3].astype(F32))
        for i in range(D0):
            lines = slice(i * SIDE, (i + 1) * SIDE)
            pad[i * WIDE + 8 : i * WIDE + 8 + SIDE] = north[lines]
            low = (D0 + SIDE + i) * WIDE + 8
            pad[low : low + SIDE] = south[lines]
            pad[pl.ds(D0 * WIDE + 8 - D0 + i, SIDE, stride=WIDE), :] = west[lines]
            pad[pl.ds(D0 * WIDE + 8 + SIDE + i, SIDE, stride=WIDE), :] = east[lines]
        for k, (r, c) in enumerate(((0, 8 - D0), (0, 8 + SIDE), (D0 + SIDE, 8 - D0), (D0 + SIDE, 8 + SIDE))):
            stage_f[...] = change(corners[k].astype(F32))
            for i in range(D0):
                start = (r + i) * WIDE + c
                pad[start : start + D0] = stage_f[i * D0 : (i + 1) * D0]

    def fill_centre(tile, pad, dilation, change):
        for i in range(SIDE):
            start = (dilation + i) * WIDE + 8
            pad[start : start + SIDE] = change(tile[i * SIDE : (i + 1) * SIDE])

    def pack_wide(tile, edges, corners):
        for k, first in ((0, 0), (1, SIDE - D1)):
            edges[k] = jnp.concatenate(
                [tile[i * SIDE + first : i * SIDE + first + D1] for i in range(SIDE)], axis=0
            ).astype(BF16)
        for k, (r, c) in enumerate(((0, 0), (0, SIDE - D1), (SIDE - D1, 0), (SIDE - D1, SIDE - D1))):
            corners[k] = jnp.concatenate(
                [tile[(r + i) * SIDE + c : (r + i) * SIDE + c + D1] for i in range(D1)], axis=0
            ).astype(BF16)

    def wide_sources(flat, edges, corners):
        lines = D1 * SIDE
        return (
            flat.at[0:lines],
            flat.at[AREA - lines : AREA],
            edges.at[0],
            edges.at[1],
        ) + tuple(corners.at[k] for k in range(4))

    def unpack_wide(edges, corners, pad):
        north = edges[0].astype(F32)
        south = edges[1].astype(F32)
        west = edges[2].astype(F32)
        east = edges[3].astype(F32)
        for i in range(D1):
            lines = slice(i * SIDE, (i + 1) * SIDE)
            pad[i * WIDE + D1 : i * WIDE + D1 + SIDE] = north[lines]
            low = (D1 + SIDE + i) * WIDE + D1
            pad[low : low + SIDE] = south[lines]
        for i in range(SIDE):
            lines = slice(i * D1, (i + 1) * D1)
            start = (D1 + i) * WIDE
            pad[start : start + D1] = west[lines]
            pad[start + D1 + SIDE : start + WIDE] = east[lines]
        for k, (r, c) in enumerate(((0, 0), (0, D1 + SIDE), (D1 + SIDE, 0), (D1 + SIDE, D1 + SIDE))):
            corner = corners[k].astype(F32)
            for i in range(D1):
                start = (r + i) * WIDE + c
                pad[start : start + D1] = corner[i * D1 : (i + 1) * D1]

    def spread(pad, cols, dilation):
        for b in range(3):
            first = 8 + (b - 1) * dilation
            for i in range(0, SIDE + 2 * dilation, 2):
                two = jnp.concatenate(
                    [pad[(i + h) * WIDE + first : (i + h) * WIDE + first + SIDE] for h in range(2)], axis=0
                )
                cols[i * SIDE : (i + 2) * SIDE, b * C : (b + 1) * C] = two.astype(BF16)

    same = lambda x: x
    relu = lambda x: jnp.maximum(x, 0.0)

    fill_centre(own_f, pad_a, D0, relu)
    for ref in (first, back1, back0, proj_pad):
        ref[...] = jnp.zeros_like(ref)
    weights_copy.wait_recv()

    proj_pad[0:K] = weights[0, PROJ_ROW : PROJ_ROW + K]
    for s in range(2):
        for h in range(2):
            proj_twice[s, h * K : (h + 1) * K] = weights[s, PROJ_ROW : PROJ_ROW + K]
    tap = lambda a, b: slice((3 * a + b) * K, (3 * a + b + 1) * K)
    for a in range(3):
        for b in range(3):
            lanes = slice(b * C, (b + 1) * C)
            own, turned = slice(b * C, b * C + K), slice(b * C + K, (b + 1) * C)
            first[a, 0:K, lanes] = weights[0, tap(a, b)]
            second[a, 0:K, lanes] = weights[1, tap(a, b)]
            second[a, K : 2 * K, lanes] = weights[1, tap(b, a)]
            back0[a, own] = weights[0, tap(2 - a, 2 - b)]
            back1[a, own, 0:C] = weights[1, tap(2 - a, 2 - b)]
            back1[a, turned, C : 2 * C] = weights[1, tap(2 - b, 2 - a)]

    halo_wait(*halo0)
    unpack_narrow(recv_e0, recv_c0, pad_a, relu)
    spread(pad_a, cols_a, D0)

    chunk = 192
    shift0 = D0 * SIDE
    shift1 = D1 * SIDE

    def rows_at(base, extra=0):
        return pl.ds(pl.multiple_of(base + extra, 16), chunk)

    bias0 = weights[0, BIAS_ROW : BIAS_ROW + 16].astype(F32)[0:1]
    bias1 = weights[1, BIAS_ROW : BIAS_ROW + 16].astype(F32)[0:1]

    @pl.loop(0, AREA // chunk)
    def _(i):
        base = i * chunk
        total = bias0
        for a in range(3):
            total = total + dot(cols_a[rows_at(base, a * shift0), :], first[a], NT)
        pre0[rows_at(base), :] = total
        bottle = jnp.maximum(total, 0.0).astype(BF16)
        bottle0[rows_at(base), :] = bottle
        branch_sum = (own_f[rows_at(base), :] + dot(bottle, proj_pad[...])).astype(BF16)
        work_f[rows_at(base), :] = branch_sum.astype(F32)

    turn(work_f, sum_t)
    mirror_start(sum_t, sum_m, 0)

    mirror_wait(cot_t, cot_m, 1)

    @pl.loop(0, AREA // chunk)
    def _(i):
        at = rows_at(i * chunk)
        branch = ((cot[at, :].astype(F32) + cot_m[at, :].astype(F32)) * 0.5).astype(BF16)
        branch1[at, :] = branch
        grad_bot[at, :] = dot(branch, proj_twice[1], NT)

    mirror_wait(sum_t, sum_m, 0)

    @pl.loop(0, AREA // chunk)
    def _(i):
        at = rows_at(i * chunk)
        sym = ((work_f[at, :] + sum_m[at, :].astype(F32)) * 0.5).astype(BF16)
        live = jnp.maximum(sym, jnp.zeros_like(sym))
        hidden1[at, :] = live
        work_f[at, :] = live.astype(F32)

    pack_wide(work_f, hid_e, hid_c)
    halo1 = (1, wide_sources(hidden1, hid_e, hid_c), recv_e1, recv_c1)
    halo_start(*halo1)
    fill_centre(work_f, pad_8, D1, same)

    halo_wait(*halo1)

    pl.semaphore_signal(partner, inc=1, device_id=sibling, device_id_type=MESH)

    unpack_wide(recv_e1, recv_c1, pad_8)
    spread(pad_8, cols_8, D1)

    @pl.loop(0, AREA // chunk)
    def _(i):
        base = i * chunk
        total = bias1
        for a in range(3):
            total = total + dot(cols_8[rows_at(base, a * shift1), :], second[a], NT)
        bottle1[rows_at(base), :] = jnp.maximum(total, 0.0).astype(BF16)
        grad = jnp.where(total > 0, grad_bot[rows_at(base), :], 0.0)
        work_f[rows_at(base), :] = grad
        gp1[rows_at(base), :] = grad.astype(BF16)

    pack_wide(work_f, gp1_e, gp1_c)
    halo2 = (2, wide_sources(gp1, gp1_e, gp1_c), recv_e2, recv_c2)
    halo_start(*halo2)

    ones = jnp.ones((AREA, C), BF16)

    def weight_gradients(s, grad_pre, cols, shift, bottle, branch):
        turned_grad = grad_pre[...].T[0:K]
        for a in range(3):
            product = dot(turned_grad, cols[a * shift : a * shift + AREA, :])
            for b in range(3):
                at = (3 * a + b) * K
                grads[s, at : at + K] = product[:, b * C : (b + 1) * C].astype(BF16)
        grads[s, 9 * K : 10 * K] = dot(bottle[...].T[0:K], branch[...]).astype(BF16)
        grads[s, 10 * K : 11 * K] = dot(turned_grad, ones).astype(BF16)
        grads[s, 11 * K : 12 * K] = jnp.zeros((K, C), BF16)

    def piece_at(index):
        return pl.ds(pl.multiple_of(index * piece, 16), piece)

    slot_me = seg * n + plane_me

    def group_copy(src, dst, send_sem, recv_sem, device):
        return pltpu.make_async_remote_copy(
            src_ref=src, dst_ref=dst, send_sem=send_sem, recv_sem=recv_sem, device_id=device, device_id_type=MESH
        )

    def plane_copy(s, step):
        to = (plane_me + step) % n
        return group_copy(
            grads.at[s, piece_at(to)],
            plane_recv.at[slot_me],
            plane_send_sem.at[s, step],
            plane_recv_sem.at[slot_me],
            plane_peer(s, to),
        )

    def plane_start(s):
        @pl.when(seg != s)
        def _():
            plane_copy(s, 0).start()

        pl.loop(1, n)(lambda step: plane_copy(s, step).start())

        @pl.when(seg == s)
        def _():
            plane_recv[slot_me] = grads[s, piece_at(plane_me), :]

    def plane_sent(s):
        @pl.when(seg != s)
        def _():
            plane_copy(s, 0).wait_send()

        pl.loop(1, n)(lambda step: plane_copy(s, step).wait_send())

    def plane_wait():
        @pl.loop(1, 2 * n)
        def _(step):
            slot = (slot_me + step) % (2 * n)
            group_copy(
                plane_recv.at[slot], plane_recv.at[slot], plane_send_sem.at[0, 0], plane_recv_sem.at[slot], sibling
            ).wait_recv()

    def line_copy(step):
        to = (line_me + step) % n
        return group_copy(
            line_recv.at[line_me], line_recv.at[line_me], line_send_sem.at[step], line_recv_sem.at[line_me], line_peer(to)
        )

    def all_copy(step):
        to = (plane_me + step) % n
        return group_copy(
            total_recv.at[plane_me],
            total_recv.at[plane_me],
            all_send_sem.at[step],
            all_recv_sem.at[plane_me],
            plane_peer(seg, to),
        )

    def arrivals(me, dst, send_sem, recv_sem):
        @pl.loop(1, n)
        def _(step):
            index = (me + step) % n
            group_copy(dst.at[index], dst.at[index], send_sem.at[step], recv_sem.at[index], sibling).wait_recv()

    def add_up(buffer, count):
        total = buffer[0].astype(F32)
        for i in range(1, count):
            total = total + buffer[i].astype(F32)
        return total

    def line_start():
        plane_wait()
        line_recv[line_me] = add_up(plane_recv, 2 * n).astype(BF16)
        pl.loop(1, n)(lambda step: line_copy(step).start())

    weight_gradients(1, gp1, cols_8, shift1, bottle1, branch1)
    pl.semaphore_wait(partner, 1)
    plane_start(1)
    fill_centre(work_f, pad_9, D1, same)
    pl.semaphore_wait(greeting, part - 1)

    halo_wait(*halo2)

    unpack_wide(recv_e2, recv_c2, pad_9)
    spread(pad_9, cols_g, D1)

    @pl.loop(0, AREA // chunk)
    def _(i):
        base = i * chunk
        total = None
        for a in range(3):
            term = dot(cols_g[rows_at(base, a * shift1), :], back1[a])
            total = term if total is None else total + term
        branch = branch1[rows_at(base), :].astype(F32)
        live = hidden1[rows_at(base), :].astype(F32) > 0
        own = (branch + jnp.where(live, total[:, 0:C], 0.0)).astype(BF16).astype(F32)
        turned = (branch + jnp.where(live, total[:, C : 2 * C], 0.0)).astype(BF16).astype(F32)
        mean = ((own + turned) * 0.5).astype(BF16)
        branch0[rows_at(base), :] = mean
        grad = jnp.where(pre0[rows_at(base), :] > 0, dot(mean, proj_twice[0], NT), 0.0)
        work_f[rows_at(base), :] = grad
        gp0[rows_at(base), :] = grad.astype(BF16)

    weight_gradients(0, gp0, cols_a, shift0, bottle0, branch0)

    plane_start(0)

    pack_narrow(work_f, gp0_e, gp0_c)
    sources3 = tuple(gp0_e.at[k] for k in range(4)) + tuple(gp0_c.at[k] for k in range(4))
    halo3 = (3, sources3, recv_e3, recv_c3)
    halo_start(*halo3)
    fill_centre(work_f, pad_a, D0, same)

    line_start()

    halo_wait(*halo3)

    unpack_narrow(recv_e3, recv_c3, pad_a, same)
    spread(pad_a, cols_b, D0)

    @pl.loop(0, AREA // chunk)
    def _(i):
        base = i * chunk
        total = None
        for a in range(3):
            term = dot(cols_b[rows_at(base, a * shift0), :], back0[a])
            total = term if total is None else total + term
        branch = branch0[rows_at(base), :].astype(F32)
        live = own_f[rows_at(base), :] > 0
        out_grad[rows_at(base), :] = (branch + jnp.where(live, total, 0.0)).astype(BF16)

    pl.when(off_diagonal)(lambda: mirror_copy(sum_t, sum_m, 0).wait_send())
    pl.when(off_diagonal)(lambda: mirror_copy(cot_t, cot_m, 1).wait_send())
    weights_copy.wait_send()
    for halo in (halo0, halo1, halo2, halo3):
        halo_sent(*halo)
    plane_sent(0)
    plane_sent(1)

    arrivals(line_me, line_recv, line_send_sem, line_recv_sem)

    total_recv[plane_me] = add_up(line_recv, n).astype(BF16)
    pl.loop(1, n)(lambda step: all_copy(step).start())
    pl.loop(1, n)(lambda step: line_copy(step).wait_send())

    arrivals(plane_me, total_recv, all_send_sem, all_recv_sem)

    for i in range(n):
        values = total_recv[i].astype(F32) * factor
        if piece <= K and (i + 1) * piece <= CONV_ROWS:
            out_conv[i * piece : (i + 1) * piece] = values
        else:
            for first, last, out in ((0, CONV_ROWS, out_conv), (9 * K, 10 * K, out_proj), (10 * K, 11 * K, None)):
                low, high = max(first, i * piece), min(last, (i + 1) * piece)
                if low < high:
                    block = values[low - i * piece : high - i * piece]
                    if out is None:
                        work_f[low - first : high - first] = block
                    else:
                        out[low - first : high - first] = block
    out_bias[...] = work_f[0:K].T[0:1]
    pl.loop(1, n)(lambda step: all_copy(step).wait_send())


def solution(mesh):
    n = mesh.shape["row"]
    cells = mesh.shape["segment"] * (SIDE * n) * (SIDE * n)
    factor = float(np.float32(1.0) / np.sqrt(np.float32(cells)))
    piece = GRAD_ROWS // n
    vmem = pltpu.VMEM
    scratch = [
        vmem((AREA, C), BF16),
        vmem((AREA, C), BF16),
        vmem((1, K), BF16),
        vmem((2, PACK_ROWS, C), BF16),
        vmem((3, 2 * K, 3 * C), BF16),
        vmem((3, 2 * K, 3 * C), BF16),
        vmem((3, 3 * C, 2 * C), BF16),
        vmem((3, 3 * C, C), BF16),
        vmem((2 * K, C), BF16),
        vmem((2, 2 * K, C), BF16),
        vmem((AREA, C), F32),
        vmem((AREA, C), F32),
        vmem((16, C), F32),
        vmem((AREA, C), BF16),
        vmem((AREA, C), BF16),
        vmem((AREA, C), BF16),
        vmem((AREA, C), BF16),
        vmem((4, D0 * SIDE, C), BF16),
        vmem((4, 16, C), BF16),
        vmem((4, D0 * SIDE, C), BF16),
        vmem((4, 16, C), BF16),
        vmem((AREA, C), BF16),
        vmem((2, D1 * SIDE, C), BF16),
        vmem((4, D1 * D1, C), BF16),
        vmem((4, D1 * SIDE, C), BF16),
        vmem((4, D1 * D1, C), BF16),
        vmem((AREA, C), BF16),
        vmem((2, D1 * SIDE, C), BF16),
        vmem((4, D1 * D1, C), BF16),
        vmem((4, D1 * SIDE, C), BF16),
        vmem((4, D1 * D1, C), BF16),
        vmem((AREA, C), BF16),
        vmem((4, D0 * SIDE, C), BF16),
        vmem((4, 16, C), BF16),
        vmem((4, D0 * SIDE, C), BF16),
        vmem((4, 16, C), BF16),
        vmem(((SIDE + 2 * D0) * WIDE, C), F32),
        vmem(((SIDE + 2 * D1) * WIDE, C), F32),
        vmem(((SIDE + 2 * D1) * WIDE, C), F32),
        vmem(((SIDE + 2 * D0) * SIDE, 3 * C), BF16),
        vmem(((SIDE + 2 * D0) * SIDE, 3 * C), BF16),
        vmem(((SIDE + 2 * D1) * SIDE, 3 * C), BF16),
        vmem(((SIDE + 2 * D1) * SIDE, 3 * C), BF16),
        vmem((AREA, C), F32),
        vmem((AREA, C), BF16),
        vmem((AREA, C), F32),
        vmem((AREA, C), BF16),
        vmem((AREA, C), BF16),
        vmem((AREA, C), BF16),
        vmem((2, GRAD_ROWS, C), BF16),
        vmem((2 * n, piece, C), BF16),
        vmem((n, piece, C), BF16),
        vmem((n, piece, C), BF16),
        pltpu.SemaphoreType.DMA((4, 8)),
        pltpu.SemaphoreType.DMA((4, 8)),
        pltpu.SemaphoreType.DMA((4,)),
        pltpu.SemaphoreType.DMA((4,)),
        pltpu.SemaphoreType.DMA((2, n)),
        pltpu.SemaphoreType.DMA((2 * n,)),
    ] + [pltpu.SemaphoreType.DMA((n,))] * 4 + [pltpu.SemaphoreType.REGULAR] * 2 + [pltpu.SemaphoreType.DMA((5,))]

    call = pl.pallas_call(
        functools.partial(kernel, n, factor),
        out_shape=(
            jax.ShapeDtypeStruct((AREA, C), BF16),
            jax.ShapeDtypeStruct((CONV_ROWS, C), F32),
            jax.ShapeDtypeStruct((1, K), F32),
            jax.ShapeDtypeStruct((K, C), F32),
        ),
        in_specs=[pl.BlockSpec(memory_space=pltpu.HBM)] * 5,
        out_specs=[pl.BlockSpec(memory_space=pltpu.VMEM)] * 4,
        scratch_shapes=scratch,
        compiler_params=pltpu.CompilerParams(
            collective_id=0, has_side_effects=True, vmem_limit_bytes=58 * 1024 * 1024
        ),
        name="trunk",
    )

    def local(activations, cotangent, conv_weight, conv_bias, out_weight):
        grad, conv, bias, proj = call(
            activations.reshape(AREA, C),
            cotangent.reshape(AREA, C),
            jnp.swapaxes(conv_weight, 2, 3).reshape(CONV_ROWS, C),
            conv_bias,
            out_weight.reshape(K, C),
        )
        return (
            grad.reshape(1, SIDE, SIDE, C),
            jnp.swapaxes(conv.reshape(1, 9, K, C), 2, 3),
            bias,
            proj.reshape(1, K, C),
        )

    in_specs = (
        P("segment", "row", "col", None),
        P("segment", "row", "col", None),
        P("segment", None, None, None),
        P("segment", None),
        P("segment", None, None),
    )
    out_specs = (
        P("segment", "row", "col", None),
        P("segment", None, None, None),
        P("segment", None),
        P("segment", None, None),
    )
    return jax.shard_map(local, mesh=mesh, in_specs=in_specs, out_specs=out_specs, check_vma=False)
```

time: 100 us -> 95 us (0.950)
  Pallas kernels: 93 us -> 89.6 us
  local copies, waits for them, and re-layouts: 4.53 us -> 3.48 us
    pallas_call x1, Pallas kernels: 93 us -> 89.6 us  [local(): call(activations.reshape(AREA, C), cotangent.reshape(AREA, C), jnp.swapax...]
    unnamed x12 -> x10, local copies, waits for them, and re-layouts: 4.01 us -> 3.48 us
where the time goes in v2:
time: 95 us; the launch traced here: 93.7 us
  Pallas kernels  89.6 us (94%)
  local copies, waits for them, and re-layouts  3.48 us (4%)
    pallas_call x1, Pallas kernels, local(): call(activations.reshape(AREA, C), cotangent.reshape(AREA, C), jnp.swapax...  89.6 us
    unnamed x10, local copies, waits for them, and re-layouts  3.48 us

profile of v2, /device:TPU:6, one launch (start us, length us, event | category | flops | bytes accessed | tf_op | source)
XLA Modules:
  0.0 93.7 jit_solution(4724999518014152235)
XLA Ops:
  0.6 89.6 %trunk.1 = (bf16[576,128]{1,0:T(8,128)(2,1)}, f32[576,128]{1,0:T(8,128)}, f32[1,64]{1,0:T(1,128)}, f32[64,128]{1,0:T(8,128)}) custom-call(bf16[576,128]{1,0:T(8,128)(2,1)} %bitcast.13, bf16[576,128]{1,0:T(8,128)(2,1)} %bitcast.14, bf16[576,128]{1,0:T(8,128)(2,1)} %bitcast.15, bf16[1,64]{1,0:T(2,128)(2,1)} %bias_in.1, bf16[64,128]{1,0:T(8,128)(2,1)} %bitcast.17), custom_call_target="tpu_custom_call" | custom-call | tf_op jit(solution)/shard_map/trunk/pallas_call | solution.py:749
  90.2 0.0 copy-start
  90.2 1.6 %copy.13 = bf16[1,24,24,128]{3,2,1,0:T(8,128)(2,1)} copy(bf16[1,24,24,128]{3,2,1,0:T(8,128)(2,1)} %bitcast.12) | data formatting | bytes 294912
  91.8 0.0 copy-done
  91.8 0.0 copy-start.2
  91.9 0.0 copy-start.1
  91.9 0.7 copy.14
  92.6 0.0 copy-done.2
  92.6 0.5 copy.15
  93.1 0.0 copy-done.1
  93.1 0.6 copy.16
Async XLA Ops:
  90.2 1.6 %copy-start = (f32[576,128]{1,0:T(8,128)S(1)}, f32[576,128]{1,0:T(8,128)}, u32[]{:S(2)}) copy-start(f32[576,128]{1,0:T(8,128)} %get-tuple-element.9) | copy-start | bytes 884740
  91.8 0.7 copy-start.2
  91.9 1.2 %copy-start.1 = (f32[64,128]{1,0:T(8,128)S(1)}, f32[64,128]{1,0:T(8,128)}, u32[]{:S(2)}) copy-start(f32[64,128]{1,0:T(8,128)} %get-tuple-element.11) | copy-start | bytes 98308

commit v3 on v2

--- a/solution.py
+++ b/solution.py
@@ -99,7 +99,8 @@
     branch0,
     grads,
     plane_recv,
-    line_recv,
+    near_recv,
+    far_recv,
     total_recv,
     halo_send,
     halo_recv,
@@ -107,11 +108,12 @@
     pair_recv,
     plane_send_sem,
     plane_recv_sem,
-    line_send_sem,
-    line_recv_sem,
+    near_send_sem,
+    near_recv_sem,
+    far_send_sem,
+    far_recv_sem,
     all_send_sem,
     all_recv_sem,
-    greeting,
     partner,
     input_sem,
 ):
@@ -123,22 +125,30 @@
     row_hi, row_lo = row // part, row % part
     col_hi, col_lo = col // part, col % part
     plane_me = row_lo * part + col_lo
-    line_me = row_hi * part + col_hi
     off_diagonal = row != col
     mirror = (seg, col, row)
     sibling = (1 - seg, row, col)
 
-    def plane_peer(section, index):
-        return (section, row_hi * part + index // part, col_hi * part + index % part)
-
-    def line_peer(index):
-        return (seg, (index // part) * part + row_lo, (index % part) * part + col_lo)
-
-    def row_peer(step):
-        return (seg, ((row_hi + step) % part) * part + row_lo, col)
-
-    def col_peer(step):
-        return (seg, row, ((col_hi + step) % part) * part + col_lo)
+    def hops(step):
+        return sum(min(d, part - d) for d in divmod(step, part))
+
+    plane_steps = sorted(range(1, n), key=hops, reverse=True)
+
+    def plane_peer(section, step):
+        return (
+            section,
+            row_hi * part + (row_lo + step // part) % part,
+            col_hi * part + (col_lo + step % part) % part,
+        )
+
+    def plane_index(step):
+        return (row_lo + step // part) % part * part + (col_lo + step % part) % part
+
+    def near_peer(step):
+        return (seg, (row_hi + step) % part * part + row_lo, col)
+
+    def far_peer(step):
+        return (seg, row, (col_hi + step) % part * part + col_lo)
 
     def there(k):
         dr, dc = DIRECTIONS[k]
@@ -178,20 +188,12 @@
     pl.when(off_diagonal)(functools.partial(signal, mirror))
     greeted = greeted + off_diagonal.astype(jnp.int32)
     for step in range(1, part):
-        signal(col_peer(step))
-        signal(row_peer(step))
+        signal(far_peer(step))
+        signal(near_peer(step))
     for k in range(7, -1, -1):
         pl.when(there(k))(functools.partial(signal, neighbour(k)))
         greeted = greeted + there(k).astype(jnp.int32)
     signal(sibling)
-
-    def turn(flat, out):
-        @pl.loop(0, SIDE // 2)
-        def _(i):
-            two = jnp.concatenate(
-                [flat[pl.ds(2 * i, SIDE, stride=SIDE), :], flat[pl.ds(2 * i + 1, SIDE, stride=SIDE), :]], axis=0
-            )
-            out[pl.ds(pl.multiple_of(i * 2 * SIDE, 16), 2 * SIDE), :] = two.astype(BF16)
 
     strip = D0 * SIDE
     corners_of_tile = ((0, 0), (0, SIDE - D0), (SIDE - D0, 0), (SIDE - D0, SIDE - D0))
@@ -212,16 +214,9 @@
             edges[k] = jnp.concatenate(columns, axis=0).astype(BF16)
         pack_corners(tile, corners)
 
-    for copy in inputs:
-        copy.wait()
+    inputs[0].wait()
     own_f[...] = act[...].astype(F32)
     pack_narrow(own_f, send_e0, send_c0)
-    bias_row = bias_w[...].astype(F32)
-    weights[seg, BIAS_ROW : BIAS_ROW + 16] = jnp.broadcast_to(
-        jnp.concatenate([bias_row, bias_row], axis=1), (16, 2 * K)
-    ).astype(BF16)
-    work_f[...] = cot[...].astype(F32)
-    turn(work_f, cot_t)
 
     pl.semaphore_wait(barrier, greeted)
 
@@ -297,12 +292,28 @@
     sources0 = tuple(send_e0.at[k] for k in range(4)) + tuple(send_c0.at[k] for k in range(4))
     halo0 = (0, sources0, recv_e0, recv_c0)
     halo_start(*halo0)
+
+    def turn(flat, out):
+        @pl.loop(0, SIDE // 2)
+        def _(i):
+            two = jnp.concatenate(
+                [flat[pl.ds(2 * i, SIDE, stride=SIDE), :], flat[pl.ds(2 * i + 1, SIDE, stride=SIDE), :]], axis=0
+            )
+            out[pl.ds(pl.multiple_of(i * 2 * SIDE, 16), 2 * SIDE), :] = two.astype(BF16)
+
+    inputs[1].wait()
+    work_f[...] = cot[...].astype(F32)
+    turn(work_f, cot_t)
+    mirror_start(cot_t, cot_m, 1)
+
+    for copy in inputs[2:]:
+        copy.wait()
+    bias_row = bias_w[...].astype(F32)
+    weights[seg, BIAS_ROW : BIAS_ROW + 16] = jnp.broadcast_to(
+        jnp.concatenate([bias_row, bias_row], axis=1), (16, 2 * K)
+    ).astype(BF16)
     weights_copy = pair_copy(weights.at[seg], weights.at[seg], 2, sibling)
     weights_copy.start()
-    mirror_start(cot_t, cot_m, 1)
-    for step in range(1, part):
-        pl.semaphore_signal(greeting, inc=1, device_id=row_peer(step), device_id_type=MESH)
-
     halo_clear(*halo0)
     halo_clear(1, None, recv_e1, recv_c1)
     halo_clear(2, None, recv_e2, recv_c2)
@@ -503,62 +514,53 @@
         )
 
     def plane_copy(s, step):
-        to = (plane_me + step) % n
         return group_copy(
-            grads.at[s, piece_at(to)],
+            grads.at[s, piece_at(plane_index(step))],
             plane_recv.at[slot_me],
             plane_send_sem.at[s, step],
             plane_recv_sem.at[slot_me],
-            plane_peer(s, to),
+            plane_peer(s, step),
         )
 
     def plane_start(s):
+        for step in plane_steps:
+            plane_copy(s, step).start()
+
         @pl.when(seg != s)
         def _():
             plane_copy(s, 0).start()
 
-        pl.loop(1, n)(lambda step: plane_copy(s, step).start())
-
         @pl.when(seg == s)
         def _():
             plane_recv[slot_me] = grads[s, piece_at(plane_me), :]
 
     def plane_sent(s):
+        for step in plane_steps:
+            plane_copy(s, step).wait_send()
+
         @pl.when(seg != s)
         def _():
             plane_copy(s, 0).wait_send()
 
-        pl.loop(1, n)(lambda step: plane_copy(s, step).wait_send())
+    def arrive(dst, send_sem, recv_sem, index):
+        group_copy(dst.at[index], dst.at[index], send_sem, recv_sem.at[index], sibling).wait_recv()
 
     def plane_wait():
         @pl.loop(1, 2 * n)
         def _(step):
-            slot = (slot_me + step) % (2 * n)
-            group_copy(
-                plane_recv.at[slot], plane_recv.at[slot], plane_send_sem.at[0, 0], plane_recv_sem.at[slot], sibling
-            ).wait_recv()
-
-    def line_copy(step):
-        to = (line_me + step) % n
-        return group_copy(
-            line_recv.at[line_me], line_recv.at[line_me], line_send_sem.at[step], line_recv_sem.at[line_me], line_peer(to)
-        )
+            arrive(plane_recv, plane_send_sem.at[0, 0], plane_recv_sem, (slot_me + step) % (2 * n))
+
+    def near_copy(step):
+        mine = near_recv.at[row_hi]
+        return group_copy(mine, mine, near_send_sem.at[step], near_recv_sem.at[row_hi], near_peer(step))
+
+    def far_copy(step):
+        mine = far_recv.at[col_hi]
+        return group_copy(mine, mine, far_send_sem.at[step], far_recv_sem.at[col_hi], far_peer(step))
 
     def all_copy(step):
-        to = (plane_me + step) % n
-        return group_copy(
-            total_recv.at[plane_me],
-            total_recv.at[plane_me],
-            all_send_sem.at[step],
-            all_recv_sem.at[plane_me],
-            plane_peer(seg, to),
-        )
-
-    def arrivals(me, dst, send_sem, recv_sem):
-        @pl.loop(1, n)
-        def _(step):
-            index = (me + step) % n
-            group_copy(dst.at[index], dst.at[index], send_sem.at[step], recv_sem.at[index], sibling).wait_recv()
+        mine = total_recv.at[plane_me]
+        return group_copy(mine, mine, all_send_sem.at[step], all_recv_sem.at[plane_me], plane_peer(seg, step))
 
     def add_up(buffer, count):
         total = buffer[0].astype(F32)
@@ -566,16 +568,23 @@
             total = total + buffer[i].astype(F32)
         return total
 
-    def line_start():
+    def near_start():
         plane_wait()
-        line_recv[line_me] = add_up(plane_recv, 2 * n).astype(BF16)
-        pl.loop(1, n)(lambda step: line_copy(step).start())
+        near_recv[row_hi] = add_up(plane_recv, 2 * n).astype(BF16)
+        for step in range(1, part):
+            near_copy(step).start()
+
+    def far_start():
+        for step in range(1, part):
+            arrive(near_recv, near_send_sem.at[step], near_recv_sem, (row_hi + step) % part)
+        far_recv[col_hi] = add_up(near_recv, part).astype(BF16)
+        for step in range(1, part):
+            far_copy(step).start()
 
     weight_gradients(1, gp1, cols_8, shift1, bottle1, branch1)
     pl.semaphore_wait(partner, 1)
     plane_start(1)
     fill_centre(work_f, pad_9, D1, same)
-    pl.semaphore_wait(greeting, part - 1)
 
     halo_wait(*halo2)
 
@@ -609,7 +618,9 @@
     halo_start(*halo3)
     fill_centre(work_f, pad_a, D0, same)
 
-    line_start()
+    near_start()
+
+    far_start()
 
     halo_wait(*halo3)
 
@@ -635,13 +646,19 @@
     plane_sent(0)
     plane_sent(1)
 
-    arrivals(line_me, line_recv, line_send_sem, line_recv_sem)
-
-    total_recv[plane_me] = add_up(line_recv, n).astype(BF16)
-    pl.loop(1, n)(lambda step: all_copy(step).start())
-    pl.loop(1, n)(lambda step: line_copy(step).wait_send())
-
-    arrivals(plane_me, total_recv, all_send_sem, all_recv_sem)
+    for step in range(1, part):
+        arrive(far_recv, far_send_sem.at[step], far_recv_sem, (col_hi + step) % part)
+
+    total_recv[plane_me] = add_up(far_recv, part).astype(BF16)
+    for step in plane_steps:
+        all_copy(step).start()
+    for step in range(1, part):
+        near_copy(step).wait_send()
+        far_copy(step).wait_send()
+
+    @pl.loop(1, n)
+    def _(step):
+        arrive(total_recv, all_send_sem.at[step], all_recv_sem, (plane_me + step) % n)
 
     for i in range(n):
         values = total_recv[i].astype(F32) * factor
@@ -657,7 +674,8 @@
                     else:
                         out[low - first : high - first] = block
     out_bias[...] = work_f[0:K].T[0:1]
-    pl.loop(1, n)(lambda step: all_copy(step).wait_send())
+    for step in plane_steps:
+        all_copy(step).wait_send()
 
 
 def solution(mesh):
@@ -665,6 +683,7 @@
     cells = mesh.shape["segment"] * (SIDE * n) * (SIDE * n)
     factor = float(np.float32(1.0) / np.sqrt(np.float32(cells)))
     piece = GRAD_ROWS // n
+    part = int(round(n**0.5))
     vmem = pltpu.VMEM
     scratch = [
         vmem((AREA, C), BF16),
@@ -718,7 +737,8 @@
         vmem((AREA, C), BF16),
         vmem((2, GRAD_ROWS, C), BF16),
         vmem((2 * n, piece, C), BF16),
-        vmem((n, piece, C), BF16),
+        vmem((part, piece, C), BF16),
+        vmem((part, piece, C), BF16),
         vmem((n, piece, C), BF16),
         pltpu.SemaphoreType.DMA((4, 8)),
         pltpu.SemaphoreType.DMA((4, 8)),
@@ -726,7 +746,8 @@
         pltpu.SemaphoreType.DMA((4,)),
         pltpu.SemaphoreType.DMA((2, n)),
         pltpu.SemaphoreType.DMA((2 * n,)),
-    ] + [pltpu.SemaphoreType.DMA((n,))] * 4 + [pltpu.SemaphoreType.REGULAR] * 2 + [pltpu.SemaphoreType.DMA((5,))]
+    ] + [pltpu.SemaphoreType.DMA((part,))] * 4 + [pltpu.SemaphoreType.DMA((n,))] * 2
+    scratch += [pltpu.SemaphoreType.REGULAR, pltpu.SemaphoreType.DMA((5,))]
 
     call = pl.pallas_call(
         functools.partial(kernel, n, factor),

time: 95 us -> 92.8 us (0.977); the launches traced: 93.7 us -> 92.6 us
  Pallas kernels: 89.6 us -> 88.5 us
    pallas_call x1, Pallas kernels: 89.6 us -> 88.5 us  [local(): call(activations.reshape(AREA, C), cotangent.reshape(AREA, C), jnp.swapax...]
where the time goes in v3:
time: 92.8 us; the launch traced here: 92.6 us
  Pallas kernels  88.5 us (95%)
  local copies, waits for them, and re-layouts  3.48 us (4%)
    pallas_call x1, Pallas kernels, local(): call(activations.reshape(AREA, C), cotangent.reshape(AREA, C), jnp.swapax...  88.5 us
    unnamed x10, local copies, waits for them, and re-layouts  3.48 us

profile of v3, /device:TPU:6, one launch (start us, length us, event | category | flops | bytes accessed | tf_op | source)
XLA Modules:
  0.0 92.6 jit_solution(10602547157705626442)
XLA Ops:
  0.6 88.5 %trunk.1 = (bf16[576,128]{1,0:T(8,128)(2,1)}, f32[576,128]{1,0:T(8,128)}, f32[1,64]{1,0:T(1,128)}, f32[64,128]{1,0:T(8,128)}) custom-call(bf16[576,128]{1,0:T(8,128)(2,1)} %bitcast.13, bf16[576,128]{1,0:T(8,128)(2,1)} %bitcast.14, bf16[576,128]{1,0:T(8,128)(2,1)} %bitcast.15, bf16[1,64]{1,0:T(2,128)(2,1)} %bias_in.1, bf16[64,128]{1,0:T(8,128)(2,1)} %bitcast.17), custom_call_target="tpu_custom_call" | custom-call | tf_op jit(solution)/shard_map/trunk/pallas_call | solution.py:770
  89.2 0.0 copy-start
  89.2 1.6 %copy.13 = bf16[1,24,24,128]{3,2,1,0:T(8,128)(2,1)} copy(bf16[1,24,24,128]{3,2,1,0:T(8,128)(2,1)} %bitcast.12) | data formatting | bytes 294912
  90.8 0.0 copy-done
  90.8 0.0 copy-start.2
  90.8 0.0 copy-start.1
  90.8 0.7 copy.14
  91.5 0.0 copy-done.2
  91.5 0.5 copy.15
  92.0 0.0 copy-done.1
  92.0 0.6 copy.16
Async XLA Ops:
  89.2 1.6 %copy-start = (f32[576,128]{1,0:T(8,128)S(1)}, f32[576,128]{1,0:T(8,128)}, u32[]{:S(2)}) copy-start(f32[576,128]{1,0:T(8,128)} %get-tuple-element.9) | copy-start | bytes 884740
  90.8 0.7 copy-start.2
  90.8 1.2 %copy-start.1 = (f32[64,128]{1,0:T(8,128)S(1)}, f32[64,128]{1,0:T(8,128)}, u32[]{:S(2)}) copy-start(f32[64,128]{1,0:T(8,128)} %get-tuple-element.11) | copy-start | bytes 98308

commit v4 on v3

--- a/solution.py
+++ b/solution.py
@@ -38,16 +38,13 @@
 
 def kernel(
     n,
-    factor,
     act_in,
     cot_in,
     conv_in,
     bias_in,
     proj_in,
     out_grad,
-    out_conv,
-    out_bias,
-    out_proj,
+    total_recv,
     act,
     cot,
     bias_w,
@@ -101,7 +98,6 @@
     plane_recv,
     near_recv,
     far_recv,
-    total_recv,
     halo_send,
     halo_recv,
     pair_send,
@@ -660,22 +656,26 @@
     def _(step):
         arrive(total_recv, all_send_sem.at[step], all_recv_sem, (plane_me + step) % n)
 
-    for i in range(n):
-        values = total_recv[i].astype(F32) * factor
-        if piece <= K and (i + 1) * piece <= CONV_ROWS:
-            out_conv[i * piece : (i + 1) * piece] = values
-        else:
-            for first, last, out in ((0, CONV_ROWS, out_conv), (9 * K, 10 * K, out_proj), (10 * K, 11 * K, None)):
-                low, high = max(first, i * piece), min(last, (i + 1) * piece)
-                if low < high:
-                    block = values[low - i * piece : high - i * piece]
-                    if out is None:
-                        work_f[low - first : high - first] = block
-                    else:
-                        out[low - first : high - first] = block
-    out_bias[...] = work_f[0:K].T[0:1]
     for step in plane_steps:
         all_copy(step).wait_send()
+
+
+def write(factor, grad, total, out_grad, out_conv, out_bias, out_proj, sums, bias, sems):
+    first = pltpu.make_async_copy(grad, out_grad, sems.at[0])
+    first.start()
+    pieces, piece = total.shape[0], total.shape[1]
+    for i in range(pieces):
+        sums[i * piece : (i + 1) * piece] = total[i].astype(F32) * factor
+    bias[...] = sums[10 * K : 11 * K].T[0:1]
+    copies = [
+        pltpu.make_async_copy(sums.at[0:CONV_ROWS], out_conv, sems.at[1]),
+        pltpu.make_async_copy(bias, out_bias, sems.at[2]),
+        pltpu.make_async_copy(sums.at[9 * K : 10 * K], out_proj, sems.at[3]),
+    ]
+    for copy in copies:
+        copy.start()
+    for copy in [first] + copies:
+        copy.wait()
 
 
 def solution(mesh):
@@ -739,7 +739,6 @@
         vmem((2 * n, piece, C), BF16),
         vmem((part, piece, C), BF16),
         vmem((part, piece, C), BF16),
-        vmem((n, piece, C), BF16),
         pltpu.SemaphoreType.DMA((4, 8)),
         pltpu.SemaphoreType.DMA((4, 8)),
         pltpu.SemaphoreType.DMA((4,)),
@@ -750,30 +749,47 @@
     scratch += [pltpu.SemaphoreType.REGULAR, pltpu.SemaphoreType.DMA((5,))]
 
     call = pl.pallas_call(
-        functools.partial(kernel, n, factor),
+        functools.partial(kernel, n),
+        out_shape=(
+            jax.ShapeDtypeStruct((AREA, C), BF16),
+            jax.ShapeDtypeStruct((n, piece, C), BF16),
+        ),
+        in_specs=[pl.BlockSpec(memory_space=pltpu.HBM)] * 5,
+        out_specs=[pl.BlockSpec(memory_space=pltpu.VMEM)] * 2,
+        scratch_shapes=scratch,
+        compiler_params=pltpu.CompilerParams(
+            collective_id=0, has_side_effects=True, vmem_limit_bytes=40 * 1024 * 1024
+        ),
+        name="trunk",
+    )
+
+    finish = pl.pallas_call(
+        functools.partial(write, factor),
         out_shape=(
             jax.ShapeDtypeStruct((AREA, C), BF16),
             jax.ShapeDtypeStruct((CONV_ROWS, C), F32),
             jax.ShapeDtypeStruct((1, K), F32),
             jax.ShapeDtypeStruct((K, C), F32),
         ),
-        in_specs=[pl.BlockSpec(memory_space=pltpu.HBM)] * 5,
-        out_specs=[pl.BlockSpec(memory_space=pltpu.VMEM)] * 4,
-        scratch_shapes=scratch,
-        compiler_params=pltpu.CompilerParams(
-            collective_id=0, has_side_effects=True, vmem_limit_bytes=58 * 1024 * 1024
-        ),
-        name="trunk",
+        in_specs=[pl.BlockSpec(memory_space=pltpu.VMEM)] * 2,
+        out_specs=[pl.BlockSpec(memory_space=pltpu.HBM)] * 4,
+        scratch_shapes=[vmem((GRAD_ROWS, C), F32), vmem((1, K), F32), pltpu.SemaphoreType.DMA((4,))],
+        compiler_params=pltpu.CompilerParams(vmem_limit_bytes=8 * 1024 * 1024),
+        name="outputs",
     )
 
     def local(activations, cotangent, conv_weight, conv_bias, out_weight):
-        grad, conv, bias, proj = call(
-            activations.reshape(AREA, C),
-            cotangent.reshape(AREA, C),
-            jnp.swapaxes(conv_weight, 2, 3).reshape(CONV_ROWS, C),
-            conv_bias,
-            out_weight.reshape(K, C),
-        )
+        held = [
+            pltpu.with_memory_space_constraint(x, pltpu.HBM)
+            for x in (
+                activations.reshape(AREA, C),
+                cotangent.reshape(AREA, C),
+                jnp.swapaxes(conv_weight, 2, 3).reshape(CONV_ROWS, C),
+                conv_bias,
+                out_weight.reshape(K, C),
+            )
+        ]
+        grad, conv, bias, proj = finish(*call(*held))
         return (
             grad.reshape(1, SIDE, SIDE, C),
             jnp.swapaxes(conv.reshape(1, 9, K, C), 2, 3),

time: 92.8 us -> 89.3 us (0.962)
  local copies, waits for them, and re-layouts: 3.48 us -> 0 us
    unnamed x10 -> x0, local copies, waits for them, and re-layouts: 3.48 us -> none
    pallas_call x1 -> x2, Pallas kernels: 88.5 us -> 88.5 us  [local(): grad, conv, bias, proj = finish(*call(*held))]
where the time goes in v4:
time: 89.3 us; the launch traced here: 89.1 us
  Pallas kernels  88.5 us (99%)
    pallas_call x2, Pallas kernels, local(): grad, conv, bias, proj = finish(*call(*held))  88.5 us

profile of v4, /device:TPU:6, one launch (start us, length us, event | category | flops | bytes accessed | tf_op | source)
XLA Modules:
  0.0 89.1 jit_solution(14091052331715516273)
XLA Ops:
  0.6 87.7 %trunk.1 = (bf16[576,128]{1,0:T(8,128)(2,1)S(1)}, bf16[16,48,128]{2,1,0:T(8,128)(2,1)S(1)}) custom-call(bf16[576,128]{1,0:T(8,128)(2,1)} %bitcast.11, bf16[576,128]{1,0:T(8,128)(2,1)} %bitcast.12, bf16[576,128]{1,0:T(8,128)(2,1)} %bitcast.13, bf16[1,64]{1,0:T(2,128)(2,1)} %bias_in.1, bf16[64,128]{1,0:T(8,128)(2,1)} %bitcast.14), custom_call_target="tpu_custom_call" | custom-call | tf_op jit(solution)/shard_map/trunk/pallas_call | solution.py:792
  88.3 0.8 outputs.1

commit v5 on v4

--- a/solution.py
+++ b/solution.py
@@ -300,7 +300,7 @@
     inputs[1].wait()
     work_f[...] = cot[...].astype(F32)
     turn(work_f, cot_t)
-    mirror_start(cot_t, cot_m, 1)
+    mirror_start(cot_t.at[0:288], cot_m.at[0:288], 1)
 
     for copy in inputs[2:]:
         copy.wait()
@@ -439,15 +439,7 @@
 
     turn(work_f, sum_t)
     mirror_start(sum_t, sum_m, 0)
-
-    mirror_wait(cot_t, cot_m, 1)
-
-    @pl.loop(0, AREA // chunk)
-    def _(i):
-        at = rows_at(i * chunk)
-        branch = ((cot[at, :].astype(F32) + cot_m[at, :].astype(F32)) * 0.5).astype(BF16)
-        branch1[at, :] = branch
-        grad_bot[at, :] = dot(branch, proj_twice[1], NT)
+    mirror_start(cot_t.at[288:AREA], cot_m.at[288:AREA], 3)
 
     mirror_wait(sum_t, sum_m, 0)
 
@@ -463,6 +455,16 @@
     halo1 = (1, wide_sources(hidden1, hid_e, hid_c), recv_e1, recv_c1)
     halo_start(*halo1)
     fill_centre(work_f, pad_8, D1, same)
+
+    mirror_wait(cot_t.at[0:288], cot_m.at[0:288], 1)
+    mirror_wait(cot_t.at[288:AREA], cot_m.at[288:AREA], 3)
+
+    @pl.loop(0, AREA // chunk)
+    def _(i):
+        at = rows_at(i * chunk)
+        branch = ((cot[at, :].astype(F32) + cot_m[at, :].astype(F32)) * 0.5).astype(BF16)
+        branch1[at, :] = branch
+        grad_bot[at, :] = dot(branch, proj_twice[1], NT)
 
     halo_wait(*halo1)
 
@@ -635,7 +637,8 @@
         out_grad[rows_at(base), :] = (branch + jnp.where(live, total, 0.0)).astype(BF16)
 
     pl.when(off_diagonal)(lambda: mirror_copy(sum_t, sum_m, 0).wait_send())
-    pl.when(off_diagonal)(lambda: mirror_copy(cot_t, cot_m, 1).wait_send())
+    pl.when(off_diagonal)(lambda: mirror_copy(cot_t.at[0:288], cot_m.at[0:288], 1).wait_send())
+    pl.when(off_diagonal)(lambda: mirror_copy(cot_t.at[288:AREA], cot_m.at[288:AREA], 3).wait_send())
     weights_copy.wait_send()
     for halo in (halo0, halo1, halo2, halo3):
         halo_sent(*halo)

time: 89.3 us -> 87.7 us (0.982)
  Pallas kernels: 88.5 us -> 86 us
    pallas_call x2, Pallas kernels: 88.5 us -> 86 us  [local(): grad, conv, bias, proj = finish(*call(*held))]
where the time goes in v5:
time: 87.7 us; the launch traced here: 86.7 us
  Pallas kernels  86 us (98%)
    pallas_call x2, Pallas kernels, local(): grad, conv, bias, proj = finish(*call(*held))  86 us

profile of v5, /device:TPU:6, one launch (start us, length us, event | category | flops | bytes accessed | tf_op | source)
XLA Modules:
  0.0 86.7 jit_solution(17916182016781330954)
XLA Ops:
  0.6 85.2 %trunk.1 = (bf16[576,128]{1,0:T(8,128)(2,1)S(1)}, bf16[16,48,128]{2,1,0:T(8,128)(2,1)S(1)}) custom-call(bf16[576,128]{1,0:T(8,128)(2,1)} %bitcast.11, bf16[576,128]{1,0:T(8,128)(2,1)} %bitcast.12, bf16[576,128]{1,0:T(8,128)(2,1)} %bitcast.13, bf16[1,64]{1,0:T(2,128)(2,1)} %bias_in.1, bf16[64,128]{1,0:T(8,128)(2,1)} %bitcast.14), custom_call_target="tpu_custom_call" | custom-call | tf_op jit(solution)/shard_map/trunk/pallas_call | solution.py:795
  85.9 0.8 outputs.1

commit v6 on v5

--- a/solution.py
+++ b/solution.py
@@ -122,6 +122,7 @@
     col_hi, col_lo = col // part, col % part
     plane_me = row_lo * part + col_lo
     off_diagonal = row != col
+    short = jnp.logical_and(row_hi - col_hi <= 1, col_hi - row_hi <= 1)
     mirror = (seg, col, row)
     sibling = (1 - seg, row, col)
 
@@ -300,7 +301,8 @@
     inputs[1].wait()
     work_f[...] = cot[...].astype(F32)
     turn(work_f, cot_t)
-    mirror_start(cot_t.at[0:288], cot_m.at[0:288], 1)
+    pl.when(short)(lambda: mirror_start(cot_t.at[0:288], cot_m.at[0:288], 1))
+    pl.when(short)(lambda: mirror_start(cot_t.at[288:AREA], cot_m.at[288:AREA], 3))
 
     for copy in inputs[2:]:
         copy.wait()
@@ -415,7 +417,7 @@
     unpack_narrow(recv_e0, recv_c0, pad_a, relu)
     spread(pad_a, cols_a, D0)
 
-    chunk = 192
+    chunk = 288
     shift0 = D0 * SIDE
     shift1 = D1 * SIDE
 
@@ -439,7 +441,8 @@
 
     turn(work_f, sum_t)
     mirror_start(sum_t, sum_m, 0)
-    mirror_start(cot_t.at[288:AREA], cot_m.at[288:AREA], 3)
+    pl.when(jnp.logical_not(short))(lambda: mirror_start(cot_t.at[0:288], cot_m.at[0:288], 1))
+    pl.when(jnp.logical_not(short))(lambda: mirror_start(cot_t.at[288:AREA], cot_m.at[288:AREA], 3))
 
     mirror_wait(sum_t, sum_m, 0)
 

time: 87.7 us -> 85.8 us (0.978)
  Pallas kernels: 86 us -> 84.9 us
    pallas_call x2, Pallas kernels: 86 us -> 84.9 us  [local(): grad, conv, bias, proj = finish(*call(*held))]
where the time goes in v6:
time: 85.8 us; the launch traced here: 85.6 us
  Pallas kernels  84.9 us (99%)
    pallas_call x2, Pallas kernels, local(): grad, conv, bias, proj = finish(*call(*held))  84.9 us

profile of v6, /device:TPU:6, one launch (start us, length us, event | category | flops | bytes accessed | tf_op | source)
XLA Modules:
  0.0 85.6 jit_solution(393803761048789456)
XLA Ops:
  0.6 84.1 %trunk.1 = (bf16[576,128]{1,0:T(8,128)(2,1)S(1)}, bf16[16,48,128]{2,1,0:T(8,128)(2,1)S(1)}) custom-call(bf16[576,128]{1,0:T(8,128)(2,1)} %bitcast.11, bf16[576,128]{1,0:T(8,128)(2,1)} %bitcast.12, bf16[576,128]{1,0:T(8,128)(2,1)} %bitcast.13, bf16[1,64]{1,0:T(2,128)(2,1)} %bias_in.1, bf16[64,128]{1,0:T(8,128)(2,1)} %bitcast.14), custom_call_target="tpu_custom_call" | custom-call | tf_op jit(solution)/shard_map/trunk/pallas_call | solution.py:798
  84.7 0.8 outputs.1

commit v7 on v6

--- a/solution.py
+++ b/solution.py
@@ -301,8 +301,7 @@
     inputs[1].wait()
     work_f[...] = cot[...].astype(F32)
     turn(work_f, cot_t)
-    pl.when(short)(lambda: mirror_start(cot_t.at[0:288], cot_m.at[0:288], 1))
-    pl.when(short)(lambda: mirror_start(cot_t.at[288:AREA], cot_m.at[288:AREA], 3))
+    pl.when(short)(lambda: mirror_start(cot_t, cot_m, 1))
 
     for copy in inputs[2:]:
         copy.wait()
@@ -441,8 +440,7 @@
 
     turn(work_f, sum_t)
     mirror_start(sum_t, sum_m, 0)
-    pl.when(jnp.logical_not(short))(lambda: mirror_start(cot_t.at[0:288], cot_m.at[0:288], 1))
-    pl.when(jnp.logical_not(short))(lambda: mirror_start(cot_t.at[288:AREA], cot_m.at[288:AREA], 3))
+    pl.when(jnp.logical_not(short))(lambda: mirror_start(cot_t, cot_m, 1))
 
     mirror_wait(sum_t, sum_m, 0)
 
@@ -459,8 +457,7 @@
     halo_start(*halo1)
     fill_centre(work_f, pad_8, D1, same)
 
-    mirror_wait(cot_t.at[0:288], cot_m.at[0:288], 1)
-    mirror_wait(cot_t.at[288:AREA], cot_m.at[288:AREA], 3)
+    mirror_wait(cot_t, cot_m, 1)
 
     @pl.loop(0, AREA // chunk)
     def _(i):
@@ -640,8 +637,7 @@
         out_grad[rows_at(base), :] = (branch + jnp.where(live, total, 0.0)).astype(BF16)
 
     pl.when(off_diagonal)(lambda: mirror_copy(sum_t, sum_m, 0).wait_send())
-    pl.when(off_diagonal)(lambda: mirror_copy(cot_t.at[0:288], cot_m.at[0:288], 1).wait_send())
-    pl.when(off_diagonal)(lambda: mirror_copy(cot_t.at[288:AREA], cot_m.at[288:AREA], 3).wait_send())
+    pl.when(off_diagonal)(lambda: mirror_copy(cot_t, cot_m, 1).wait_send())
     weights_copy.wait_send()
     for halo in (halo0, halo1, halo2, halo3):
         halo_sent(*halo)

time: 85.8 us -> 85.7 us (level)
  no operation moved by 1% of the time
where the time goes in v7:
time: 85.7 us; the launch traced here: 85.5 us
  Pallas kernels  84.8 us (99%)
    pallas_call x2, Pallas kernels, local(): grad, conv, bias, proj = finish(*call(*held))  84.8 us

profile of v7, /device:TPU:6, one launch (start us, length us, event | category | flops | bytes accessed | tf_op | source)
XLA Modules:
  0.0 85.5 jit_solution(15752933460049584198)
XLA Ops:
  0.6 84.0 %trunk.1 = (bf16[576,128]{1,0:T(8,128)(2,1)S(1)}, bf16[16,48,128]{2,1,0:T(8,128)(2,1)S(1)}) custom-call(bf16[576,128]{1,0:T(8,128)(2,1)} %bitcast.11, bf16[576,128]{1,0:T(8,128)(2,1)} %bitcast.12, bf16[576,128]{1,0:T(8,128)(2,1)} %bitcast.13, bf16[1,64]{1,0:T(2,128)(2,1)} %bias_in.1, bf16[64,128]{1,0:T(8,128)(2,1)} %bitcast.14), custom_call_target="tpu_custom_call" | custom-call | tf_op jit(solution)/shard_map/trunk/pallas_call | solution.py:794
  84.7 0.8 outputs.1
